TPU v7x, 256 devices: a whole 4x4x8 slice. The times are simulated.
256 devices in a mesh: group: 32 (over z, y_lo, core), fsdp: 8 (over y_hi, x).
Axes of the slice: x: 4, y: 4 (y_hi: 2, y_lo: 2; y = y_hi * 2 + y_lo), z: 8, core: 2. Of those that a mesh axis runs over, the one named last changes fastest.
Arguments:
- inputs: bfloat16 [32, 4, 256, 4096], P('group', None, 'fsdp'), may hold values from -6 to 6
- cotangent: bfloat16 [32, 4, 256, 4096], P('group', None, 'fsdp'), may hold values from -6 to 6
- value_weight: bfloat16 [32, 4096, 2048], P('group', 'fsdp'), may hold values from -6 to 6
- output_weight: bfloat16 [32, 2048, 4096], P('group', 'fsdp'), may hold values from -6 to 6
- push_weight: float32 [32], P('group'), may hold values from 0.5 to 2
- position_bias: float32 [32, 32, 32], replicated, may hold values from -8 to 300
- step_index: int32 [1], replicated, may hold values from 0 to 999
Outputs:
- value_out: bfloat16 [32, 4096, 2048], P('group', 'fsdp')
- output_out: bfloat16 [32, 2048, 4096], P('group', 'fsdp')
- mass_out: float32 [32], P('group')
All inputs are finite; a program needn't handle non-finite values.
Results may differ from a plain program's by a relative error of at most 0.015.
Values may be sent and summed in bfloat16 or wider, within the bound.
A program may use at most 192 MiB of HBM per device.

v0:
```python
import math

import jax
import jax.numpy as jnp
from jax import lax
from jax.sharding import PartitionSpec as P

learn_rate = 0.5


def for_sending(array):
    return jax.tree.map(lambda a: a.astype(jnp.bfloat16) if a.dtype == jnp.float32 else a, array)


def shifted(block, axis, distance):
    devices = range(lax.axis_size(axis))
    route = [((i - distance) % len(devices), i) for i in devices]
    return lax.ppermute(block, axis, route)


def push_one(message):
    return jax.tree.map(
        lambda part, own: part.astype(own.dtype), shifted(for_sending(message), "group", 1), message
    )


def push_two(message):
    return jax.tree.map(
        lambda part, own: part.astype(own.dtype), shifted(for_sending(message), "group", 2), message
    )


def push_four(message):
    return jax.tree.map(
        lambda part, own: part.astype(own.dtype), shifted(for_sending(message), "group", 4), message
    )


def push_eight(message):
    return jax.tree.map(
        lambda part, own: part.astype(own.dtype), shifted(for_sending(message), "group", 8), message
    )


def contract_rows(left, right):
    return lax.dot_general(
        left, right, (((0,), (0,)), ((), ())), preferred_element_type=jnp.float32
    )


def on_device(
    inputs, cotangent, value_weight, output_weight, push_weight, position_bias, step_index
):
    window_steps = inputs.shape[1]
    positions = inputs.shape[2]
    model_width = inputs.shape[3]
    inner_width = value_weight.shape[2]
    head_count = position_bias.shape[0]
    head_size = inner_width // head_count
    scale_in = 1.0 / math.sqrt(model_width)
    scale_mid = 1.0 / math.sqrt(inner_width)
    attention = jax.nn.softmax(position_bias, axis=-1).astype(jnp.bfloat16)
    value_num = value_weight[0].astype(jnp.float32)
    output_num = output_weight[0].astype(jnp.float32)
    push_mass = push_weight
    pend_value = jnp.zeros(value_num.shape, jnp.bfloat16)
    pend_output = jnp.zeros(output_num.shape, jnp.bfloat16)
    pend_mass = jnp.zeros(push_mass.shape, jnp.bfloat16)
    for window_step in range(window_steps):
        eff_value = (value_num / push_mass[0]).astype(jnp.bfloat16)
        eff_output = (output_num / push_mass[0]).astype(jnp.bfloat16)
        columns = lax.all_to_all(
            inputs[0, window_step], "fsdp", split_axis=1, concat_axis=0, tiled=True
        )
        partial_value = jnp.dot(columns, eff_value, preferred_element_type=jnp.float32) * scale_in
        cot_all = lax.all_gather(cotangent[0, window_step], "fsdp", axis=0, tiled=True)
        values = lax.psum_scatter(
            partial_value.astype(jnp.bfloat16), "fsdp", scatter_dimension=0, tiled=True
        )
        mixed_rows = jnp.einsum(
            "hqk,khe->qhe",
            attention,
            values.reshape(positions, head_count, head_size),
            preferred_element_type=jnp.float32,
        )
        mixed_rows = mixed_rows.astype(jnp.bfloat16).reshape(positions, inner_width)
        mixed_cols = lax.all_to_all(mixed_rows, "fsdp", split_axis=1, concat_axis=0, tiled=True)
        dmixed_cols = (
            lax.dot_general(
                cot_all, eff_output, (((1,), (1,)), ((), ())), preferred_element_type=jnp.float32
            )
            * scale_mid
        )
        dmixed_cols = dmixed_cols.astype(jnp.bfloat16)
        dmixed = lax.all_to_all(dmixed_cols, "fsdp", split_axis=0, concat_axis=1, tiled=True)
        dvalues = jnp.einsum(
            "hqk,qhe->khe",
            attention,
            dmixed.reshape(positions, head_count, head_size),
            preferred_element_type=jnp.float32,
        )
        dvalues = dvalues.astype(jnp.bfloat16).reshape(positions, inner_width)
        dvalues_all = lax.all_gather(dvalues, "fsdp", axis=0, tiled=True)
        grad_value = contract_rows(columns, dvalues_all) * scale_in
        grad_output = contract_rows(mixed_cols, cot_all) * scale_mid
        half_value = (value_num - learn_rate * grad_value) * 0.5
        half_output = (output_num - learn_rate * grad_output) * 0.5
        half_mass = push_mass * 0.5
        message = (
            half_value.astype(jnp.bfloat16),
            half_output.astype(jnp.bfloat16),
            half_mass.astype(jnp.bfloat16),
        )
        selector = (step_index[0] + window_step) % 4
        arrived = lax.switch(selector, [push_one, push_two, push_four, push_eight], message)
        value_num = half_value + pend_value.astype(jnp.float32)
        output_num = half_output + pend_output.astype(jnp.float32)
        push_mass = half_mass + pend_mass.astype(jnp.float32)
        pend_value, pend_output, pend_mass = arrived
    value_num = value_num + pend_value.astype(jnp.float32)
    output_num = output_num + pend_output.astype(jnp.float32)
    push_mass = push_mass + pend_mass.astype(jnp.float32)
    value_out = (value_num / push_mass[0]).astype(jnp.bfloat16)[None]
    output_out = (output_num / push_mass[0]).astype(jnp.bfloat16)[None]
    return (value_out, output_out, push_mass)


def solution(mesh):
    placed = (
        P("group", None, "fsdp", None),
        P("group", None, "fsdp", None),
        P("group", "fsdp", None),
        P("group", "fsdp", None),
        P("group"),
        P(),
        P(),
    )
    return jax.shard_map(
        on_device,
        mesh=mesh,
        in_specs=placed,
        out_specs=(P("group", "fsdp", None), P("group", "fsdp", None), P("group")),
        check_vma=False,
    )
```

profile of v0, /device:TPU:6, one launch (start us, length us, event | category | flops | bytes accessed | tf_op | source)
XLA Modules:
  0.0 1260.4 jit_solution(3551202208790756364)
XLA Ops:
  36.8 36.7 %all-gather.21.cloned.1.call-done = bf16[1,1,256,4096]{3,2,1,0:T(8,128)(2,1)} async-done(((bf16[1,1,32,4096]{3,2,1,0:T(8,128)(2,1)}), bf16[1,1,256,4096]{3,2,1,0:T(8,128)(2,1)}) %all-gather.21.cloned.1.call-update) | async-done | bytes 2097168 | tf_op jit(solution)/shard_map/all_gather | solution.py:76
  82.0 71.4 %reduce-scatter.13.cloned.1.call-done = bf16[32,2048]{1,0:T(8,128)(2,1)} async-done(((bf16[256,2048]{1,0:T(8,128)(2,1)}), bf16[32,2048]{1,0:T(8,128)(2,1)}) %reduce-scatter.13.cloned.1.call-update) | async-done | bytes 131088
  174.4 41.2 %all-gather.23.cloned.1.call-done = bf16[1,1,256,4096]{3,2,1,0:T(8,128)(2,1)} async-done(((bf16[1,1,32,4096]{3,2,1,0:T(8,128)(2,1)}), bf16[1,1,256,4096]{3,2,1,0:T(8,128)(2,1)}) %all-gather.23.cloned.1.call-update) | async-done | bytes 2097168 | tf_op jit(solution)/shard_map/all_gather | solution.py:76
  237.5 32.6 %all-gather.13.cloned.1.call-done = bf16[256,2048]{1,0:T(8,128)(2,1)} async-done(((bf16[32,2048]{1,0:T(8,128)(2,1)}), bf16[256,2048]{1,0:T(8,128)(2,1)}) %all-gather.13.cloned.1.call-update) | async-done | bytes 1048592 | tf_op jit(solution)/shard_map/all_gather | solution.py:103
  288.0 37.3 %all-gather.15.cloned.1.call-done = bf16[256,2048]{1,0:T(8,128)(2,1)} async-done(((bf16[32,2048]{1,0:T(8,128)(2,1)}), bf16[256,2048]{1,0:T(8,128)(2,1)}) %all-gather.15.cloned.1.call-update) | async-done | bytes 1048592 | tf_op jit(solution)/shard_map/all_gather | solution.py:103
  331.3 67.3 %conditional.12 = (f32[256,4096]{1,0:T(8,128)}, f32[1]{0:T(128)}, f32[512,2048]{0,1:T(8,128)}) conditional(s32[]{:T(128)} %clamp.12, (bf16[512,2048]{0,1:T(8,128)(2,1)S(1)}, bf16[256,4096]{1,0:T(8,128)(2,1)}, bf16[1]{0:T(256)(128)(2,1)}) %tuple.208, (bf16[512,2048]{0,1:T(8,128)(2,1)S(1)}, ...), branch_computations={%region_3.4_spmd, %region_4.5_spmd, %region_5.6_spmd, %region_6.7_... | conditional | flops 1048577 | bytes 33554592
  335.2 46.4 %collective-permute-done.2 = bf16[1]{0:T(256)(128)(2,1)} collective-permute-done((bf16[1]{0:T(256)(128)(2,1)}, bf16[1]{0:T(256)(128)(2,1)}, u32[]{:S(2)}, u32[]{:S(2)}) %collective-permute-start.2) | collective-permute-done | bytes 34 | tf_op jit(solution)/shard_map/cond/branch_0_fun/ppermute | solution.py:18
  406.2 37.3 %reduce-scatter.15.cloned.1.call-done = bf16[32,2048]{1,0:T(8,128)(2,1)} async-done(((bf16[256,2048]{1,0:T(8,128)(2,1)}), bf16[32,2048]{1,0:T(8,128)(2,1)}) %reduce-scatter.15.cloned.1.call-update) | async-done | bytes 131088
  445.5 11.3 all_to_all.217
  462.7 42.7 %all-gather.25.cloned.1.call-done = bf16[1,1,256,4096]{3,2,1,0:T(8,128)(2,1)} async-done(((bf16[1,1,32,4096]{3,2,1,0:T(8,128)(2,1)}), bf16[1,1,256,4096]{3,2,1,0:T(8,128)(2,1)}) %all-gather.25.cloned.1.call-update) | async-done | bytes 2097168 | tf_op jit(solution)/shard_map/all_gather | solution.py:76
  510.3 10.6 all_to_all.218
  529.3 56.6 %reduce-scatter.17.cloned.1.call-done = bf16[32,2048]{1,0:T(8,128)(2,1)} async-done(((bf16[256,2048]{1,0:T(8,128)(2,1)}), bf16[32,2048]{1,0:T(8,128)(2,1)}) %reduce-scatter.17.cloned.1.call-update) | async-done | bytes 131088
  587.0 104.4 %conditional.13 = (f32[256,4096]{1,0:T(8,128)}, f32[1]{0:T(128)}, f32[512,2048]{0,1:T(8,128)}) conditional(s32[]{:T(128)} %clamp.13, (bf16[512,2048]{0,1:T(8,128)(2,1)S(1)}, bf16[256,4096]{1,0:T(8,128)(2,1)}, bf16[1]{0:T(256)(128)(2,1)}) %tuple.400, (bf16[512,2048]{0,1:T(8,128)(2,1)S(1)}, ...), branch_computations={%region_8.9_spmd, %region_9.10_spmd, %region_10.11_spmd, %region_1... | conditional | flops 1048577 | bytes 33554592
  595.7 84.8 %collective-permute-start.17 = (bf16[1]{0:T(256)(128)(2,1)}, bf16[1]{0:T(256)(128)(2,1)}, u32[]{:S(2)}, u32[]{:S(2)}) collective-permute-start(bf16[1]{0:T(256)(128)(2,1)} %get-tuple-element.185), channel_id=1, source_target_pairs={{240,0},{248,8},{0,16},{8,24},{16,32},{24,40},{32,48},{40,56},{48,... | collective-permute-start | bytes 14 | tf_op jit(solution)/shard_map/cond/branch_1_fun/ppermute | solution.py:18
  691.5 28.4 %all-gather.17.cloned.1.call-done = bf16[256,2048]{1,0:T(8,128)(2,1)} async-done(((bf16[32,2048]{1,0:T(8,128)(2,1)}), bf16[256,2048]{1,0:T(8,128)(2,1)}) %all-gather.17.cloned.1.call-update) | async-done | bytes 1048592 | tf_op jit(solution)/shard_map/all_gather | solution.py:103
  735.7 10.7 all_to_all.219
  753.6 28.0 %all-gather.27.cloned.1.call-done = bf16[1,1,256,4096]{3,2,1,0:T(8,128)(2,1)} async-done(((bf16[1,1,32,4096]{3,2,1,0:T(8,128)(2,1)}), bf16[1,1,256,4096]{3,2,1,0:T(8,128)(2,1)}) %all-gather.27.cloned.1.call-update) | async-done | bytes 2097168 | tf_op jit(solution)/shard_map/all_gather | solution.py:76
  786.6 10.6 all_to_all.220
  798.8 63.2 %reduce-scatter.19.cloned.1.call-done = bf16[32,2048]{1,0:T(8,128)(2,1)} async-done(((bf16[256,2048]{1,0:T(8,128)(2,1)}), bf16[32,2048]{1,0:T(8,128)(2,1)}) %reduce-scatter.19.cloned.1.call-update) | async-done | bytes 131088
  869.9 46.2 %all-gather.19.cloned.1.call-done = bf16[256,2048]{1,0:T(8,128)(2,1)} async-done(((bf16[32,2048]{1,0:T(8,128)(2,1)}), bf16[256,2048]{1,0:T(8,128)(2,1)}) %all-gather.19.cloned.1.call-update) | async-done | bytes 1048592 | tf_op jit(solution)/shard_map/all_gather | solution.py:103
  922.9 110.6 %conditional.14 = (f32[1]{0:T(128)}, f32[256,4096]{1,0:T(8,128)}, f32[512,2048]{0,1:T(8,128)}) conditional(s32[]{:T(128)} %clamp.14, (bf16[512,2048]{0,1:T(8,128)(2,1)}, bf16[256,4096]{1,0:T(8,128)(2,1)}, bf16[1]{0:T(256)(128)(2,1)}) %tuple.210, (bf16[512,2048]{0,1:T(8,128)(2,1)}, bf16[256,4096]{1,0:T(8,128)(2,1)}, ...), branch_computations={%region_13.14_spmd, %region_14.15_spmd, %region_15.16_spmd, %regio... | conditional | flops 1048577 | bytes 33554592
  929.9 82.9 %collective-permute-start.32 = (bf16[1]{0:T(256)(128)(2,1)}, bf16[1]{0:T(256)(128)(2,1)}, u32[]{:S(2)}, u32[]{:S(2)}) collective-permute-start(bf16[1]{0:T(256)(128)(2,1)} %get-tuple-element.200), channel_id=1, source_target_pairs={{224,0},{232,8},{240,16},{248,24},{0,32},{8,40},{16,48},{24,56},{3... | collective-permute-start | bytes 14 | tf_op jit(solution)/shard_map/cond/branch_2_fun/ppermute | solution.py:18
  1041.4 194.3 %conditional.15 = (f32[1]{0:T(128)}, f32[256,4096]{1,0:T(8,128)}, f32[512,2048]{0,1:T(8,128)}) conditional(s32[]{:T(128)} %clamp.15, (bf16[512,2048]{0,1:T(8,128)(2,1)S(1)}, bf16[256,4096]{1,0:T(8,128)(2,1)}, bf16[1]{0:T(256)(128)(2,1)}) %tuple.211, (bf16[512,2048]{0,1:T(8,128)(2,1)S(1)}, ...), branch_computations={%region_18.19_spmd, %region_19.20_spmd, %region_20.21_spmd, %regio... | conditional | flops 1048577 | bytes 33554592
  1050.0 170.6 %collective-permute-start.47 = (bf16[1]{0:T(256)(128)(2,1)}, bf16[1]{0:T(256)(128)(2,1)}, u32[]{:S(2)}, u32[]{:S(2)}) collective-permute-start(bf16[1]{0:T(256)(128)(2,1)} %get-tuple-element.215), channel_id=1, source_target_pairs={{192,0},{200,8},{208,16},{216,24},{224,32},{232,40},{240,48},{248,... | collective-permute-start | bytes 14 | tf_op jit(solution)/shard_map/cond/branch_3_fun/ppermute | solution.py:18
  (165 shorter events, 264.8 us)
Async XLA Ops:
  19.9 133.6 %reduce-scatter.13.cloned.1.call-start = ((), (), s32[]{:S(2)}) async-start(), calls=%async_computation.24 | async-start | bytes 1179648
  30.6 185.1 %all-gather.23.cloned.1.call-start = ((), (), s32[]{:S(2)}) async-start(), calls=%async_computation.21 | async-start | bytes 2359296 | tf_op jit(solution)/shard_map/all_gather | solution.py:76
  77.1 77.5 %all-to-all-start = ((bf16[8,32,256]{2,1,0:T(8,128)(2,1)}), bf16[8,32,256]{2,1,0:T(8,128)(2,1)S(1)}, u32[]{:S(2)}, u32[]{:S(2)}) async-start(bf16[8,32,256]{2,1,0:T(8,128)(2,1)} %bitcast.5), calls=%async_computation | async-start | bytes 262144 | tf_op jit(solution)/shard_map/all_to_all | solution.py:95
  81.8 188.3 %all-gather.13.cloned.1.call-start = ((), (), s32[]{:S(2)}) async-start(), calls=%async_computation.16 | async-start | bytes 1179648 | tf_op jit(solution)/shard_map/all_gather | solution.py:103
  163.0 162.3 %all-gather.15.cloned.1.call-start = ((), (), s32[]{:S(2)}) async-start(), calls=%async_computation.17 | async-start | bytes 1179648 | tf_op jit(solution)/shard_map/all_gather | solution.py:103
  237.5 206.0 %reduce-scatter.15.cloned.1.call-start = ((), (), s32[]{:S(2)}) async-start(), calls=%async_computation.25 | async-start | bytes 1179648
  281.2 224.2 %all-gather.25.cloned.1.call-start = ((), (), s32[]{:S(2)}) async-start(), calls=%async_computation.22 | async-start | bytes 2359296 | tf_op jit(solution)/shard_map/all_gather | solution.py:76
  282.8 115.7 %all-to-all-start.7 = ((bf16[32,8,512]{2,0,1:T(8,128)(2,1)}), bf16[32,8,512]{2,0,1:T(8,128)(2,1)S(1)}, u32[]{:S(2)}, u32[]{:S(2)}) async-start(bf16[32,8,512]{2,0,1:T(8,128)(2,1)} %copy.170), calls=%async_computation.7 | async-start | bytes 524288 | tf_op jit(solution)/shard_map/all_to_all | solution.py:72
  287.3 298.5 %reduce-scatter.17.cloned.1.call-start = ((), (), s32[]{:S(2)}) async-start(), calls=%async_computation.26 | async-start | bytes 1179648
  406.2 313.7 %all-gather.17.cloned.1.call-start = ((), (), s32[]{:S(2)}) async-start(), calls=%async_computation.18 | async-start | bytes 1179648 | tf_op jit(solution)/shard_map/all_gather | solution.py:103
  522.5 259.1 %all-gather.27.cloned.1.call-start = ((), (), s32[]{:S(2)}) async-start(), calls=%async_computation.23 | async-start | bytes 2359296 | tf_op jit(solution)/shard_map/all_gather | solution.py:76
  524.0 203.2 %all-to-all-start.10 = ((bf16[32,8,512]{2,0,1:T(8,128)(2,1)}), bf16[32,8,512]{2,0,1:T(8,128)(2,1)S(1)}, u32[]{:S(2)}, u32[]{:S(2)}) async-start(bf16[32,8,512]{2,0,1:T(8,128)(2,1)} %copy.183), calls=%async_computation.10 | async-start | bytes 524288 | tf_op jit(solution)/shard_map/all_to_all | solution.py:72
  529.3 332.7 %reduce-scatter.19.cloned.1.call-start = ((), (), s32[]{:S(2)}) async-start(), calls=%async_computation.27 | async-start | bytes 1179648
  590.2 93.7 %collective-permute-start.16 = (bf16[256,4096]{1,0:T(8,128)(2,1)}, bf16[256,4096]{1,0:T(8,128)(2,1)}, u32[]{:S(2)}, u32[]{:S(2)}) collective-permute-start(bf16[256,4096]{1,0:T(8,128)(2,1)} %get-tuple-element.184), channel_id=1, source_target_pairs={{240,0},{248,8},{0,16},{8,24},{16,32},{24,40},{32,48},{40,56},{48,... | collective-permute-start | bytes 6291464 | tf_op jit(solution)/shard_map/cond/branch_1_fun/ppermute | solution.py:18
  593.3 94.8 %collective-permute-start.15 = (bf16[512,2048]{1,0:T(8,128)(2,1)}, bf16[512,2048]{1,0:T(8,128)(2,1)S(1)}, u32[]{:S(2)}, u32[]{:S(2)}) collective-permute-start(bf16[512,2048]{1,0:T(8,128)(2,1)} %copy.172), channel_id=1, source_target_pairs={{240,0},{248,8},{0,16},{8,24},{16,32},{24,40},{32,48},{40,56},{48,... | collective-permute-start | bytes 6291464 | tf_op jit(solution)/shard_map/cond/branch_1_fun/ppermute | solution.py:18
  595.7 87.6 %collective-permute-start.17 = (bf16[1]{0:T(256)(128)(2,1)}, bf16[1]{0:T(256)(128)(2,1)}, u32[]{:S(2)}, u32[]{:S(2)}) collective-permute-start(bf16[1]{0:T(256)(128)(2,1)} %get-tuple-element.185), channel_id=1, source_target_pairs={{240,0},{248,8},{0,16},{8,24},{16,32},{24,40},{32,48},{40,56},{48,... | collective-permute-start | bytes 14 | tf_op jit(solution)/shard_map/cond/branch_1_fun/ppermute | solution.py:18
  734.9 181.2 %all-gather.19.cloned.1.call-start = ((), (), s32[]{:S(2)}) async-start(), calls=%async_computation.19 | async-start | bytes 1179648 | tf_op jit(solution)/shard_map/all_gather | solution.py:103
  864.6 168.9 %all-to-all-start.11 = ((bf16[32,8,256]{2,0,1:T(8,128)(2,1)}), bf16[32,8,256]{2,0,1:T(8,128)(2,1)S(1)}, u32[]{:S(2)}, u32[]{:S(2)}) async-start(bf16[32,8,256]{2,0,1:T(8,128)(2,1)} %copy.191), calls=%async_computation.11 | async-start | bytes 262144 | tf_op jit(solution)/shard_map/all_to_all | solution.py:87
  922.9 93.1 %collective-permute-start.31 = (bf16[256,4096]{1,0:T(8,128)(2,1)}, bf16[256,4096]{1,0:T(8,128)(2,1)}, u32[]{:S(2)}, u32[]{:S(2)}) collective-permute-start(bf16[256,4096]{1,0:T(8,128)(2,1)} %get-tuple-element.199), channel_id=1, source_target_pairs={{224,0},{232,8},{240,16},{248,24},{0,32},{8,40},{16,48},{24,56},{3... | collective-permute-start | bytes 6291464 | tf_op jit(solution)/shard_map/cond/branch_2_fun/ppermute | solution.py:18
  928.4 91.7 %collective-permute-start.30 = (bf16[512,2048]{1,0:T(8,128)(2,1)}, bf16[512,2048]{1,0:T(8,128)(2,1)}, u32[]{:S(2)}, u32[]{:S(2)}) collective-permute-start(bf16[512,2048]{1,0:T(8,128)(2,1)} %copy.186), channel_id=1, source_target_pairs={{224,0},{232,8},{240,16},{248,24},{0,32},{8,40},{16,48},{24,56},{3... | collective-permute-start | bytes 6291464 | tf_op jit(solution)/shard_map/cond/branch_2_fun/ppermute | solution.py:18
  929.9 85.5 %collective-permute-start.32 = (bf16[1]{0:T(256)(128)(2,1)}, bf16[1]{0:T(256)(128)(2,1)}, u32[]{:S(2)}, u32[]{:S(2)}) collective-permute-start(bf16[1]{0:T(256)(128)(2,1)} %get-tuple-element.200), channel_id=1, source_target_pairs={{224,0},{232,8},{240,16},{248,24},{0,32},{8,40},{16,48},{24,56},{3... | collective-permute-start | bytes 14 | tf_op jit(solution)/shard_map/cond/branch_2_fun/ppermute | solution.py:18
  1041.4 183.5 %collective-permute-start.46 = (bf16[256,4096]{1,0:T(8,128)(2,1)}, bf16[256,4096]{1,0:T(8,128)(2,1)}, u32[]{:S(2)}, u32[]{:S(2)}) collective-permute-start(bf16[256,4096]{1,0:T(8,128)(2,1)} %get-tuple-element.214), channel_id=1, source_target_pairs={{192,0},{200,8},{208,16},{216,24},{224,32},{232,40},{240,48},{248,... | collective-permute-start | bytes 6291464 | tf_op jit(solution)/shard_map/cond/branch_3_fun/ppermute | solution.py:18
  1045.0 184.0 %collective-permute-start.45 = (bf16[512,2048]{1,0:T(8,128)(2,1)}, bf16[512,2048]{1,0:T(8,128)(2,1)S(1)}, u32[]{:S(2)}, u32[]{:S(2)}) collective-permute-start(bf16[512,2048]{1,0:T(8,128)(2,1)} %copy.195), channel_id=1, source_target_pairs={{192,0},{200,8},{208,16},{216,24},{224,32},{232,40},{240,48},{248,... | collective-permute-start | bytes 6291464 | tf_op jit(solution)/shard_map/cond/branch_3_fun/ppermute | solution.py:18
  1050.0 174.3 %collective-permute-start.47 = (bf16[1]{0:T(256)(128)(2,1)}, bf16[1]{0:T(256)(128)(2,1)}, u32[]{:S(2)}, u32[]{:S(2)}) collective-permute-start(bf16[1]{0:T(256)(128)(2,1)} %get-tuple-element.215), channel_id=1, source_target_pairs={{192,0},{200,8},{208,16},{216,24},{224,32},{232,40},{240,48},{248,... | collective-permute-start | bytes 14 | tf_op jit(solution)/shard_map/cond/branch_3_fun/ppermute | solution.py:18
  (16 other events, 571.2 us)
Sparse Core Ops, SparseCore 0:
  10.6 62.8 all-gather.20
  77.4 75.9 reduce-scatter.12
  156.4 59.1 all-gather.22
  218.5 51.5 all-gather.12
  272.9 52.3 all-gather.14
  329.6 113.8 reduce-scatter.14
  446.2 59.1 all-gather.24
  509.3 76.5 reduce-scatter.16
  588.8 130.9 all-gather.16
  722.7 58.9 all-gather.26
  786.1 75.8 reduce-scatter.18
  864.5 51.6 all-gather.18
where the time goes:
time: 1270 us; the launch traced here: 1260 us
  waiting for transfers between devices  588 us (46%)
  starting transfers between devices  390 us (31%)
  matrix products  87.1 us (7%)
  local copies, waits for them, and re-layouts  59.2 us (5%)
  blocking collectives  53.6 us (4%)
  other arithmetic  35.7 us (3%)
  loops' own time  28.4 us (2%)
  between operations  17.8 us (1%)
    ppermute x12, starting transfers between devices, shifted(): return lax.ppermute(block, axis, route)  352 us
    unnamed x16, waiting for transfers between devices  231 us
    all_gather x4, waiting for transfers between devices, on_device(): lax.all_gather(cotangent[0, window_step], 'fsdp', axis=0, tiled=True)  149 us
    all_gather x4, waiting for transfers between devices, on_device(): dvalues_all = lax.all_gather(dvalues, 'fsdp', axis=0, tiled=True)  144 us
    ppermute x12, waiting for transfers between devices, shifted(): return lax.ppermute(block, axis, route)  55.4 us
    dot_general x8, matrix products, contract_rows(): lax.dot_general(left, right, (((0,), (0,)), ((), ())), preferred_element_...  51.3 us
    all_to_all x3, blocking collectives, on_device(): lax.all_to_all(dmixed_cols, 'fsdp', split_axis=0, concat_axis=1, tiled=True)  31.6 us
    unnamed x4, loops' own time  28.4 us
  transfers between devices with their start and end apart: 31, of which 18 were waited for; matrix products, arithmetic and copies ran while one was open for 12% of the time, Pallas kernels for 0%

commit v1 on v0

v1 whole, which is shorter than its diff:
```python
import functools
import math

import jax
import jax.numpy as jnp
from jax import lax
from jax.sharding import PartitionSpec as P

learn_rate = 0.5
DISTANCES = (1, 2, 4, 8)


def shifted(block, axis, distance):
    count = lax.axis_size(axis)
    route = [((i - distance) % count, i) for i in range(count)]
    return lax.ppermute(block, axis, route)


def contract_rows(left, right):
    return lax.dot_general(
        left, right, (((0,), (0,)), ((), ())), preferred_element_type=jnp.float32
    )


def run_window(first, columns, cot_all, attention, value_num, output_num, push_mass):
    window_steps, batch, _ = columns.shape
    heads, positions, _ = attention.shape
    inner_own = output_num.shape[0]
    head_size = inner_own // heads
    model_width = cot_all.shape[2]
    inner_width = value_num.shape[1]
    sequences = batch // positions
    scale_in = 1.0 / math.sqrt(model_width)
    scale_mid = 1.0 / math.sqrt(inner_width)
    arrived = None
    for step in range(window_steps):
        distance = DISTANCES[(first + step) % 4]
        eff_value = (value_num / push_mass[0]).astype(jnp.bfloat16)
        eff_output = (output_num / push_mass[0]).astype(jnp.bfloat16)
        cols = columns[step]
        cot = cot_all[step]
        dmixed = (
            lax.dot_general(
                cot, eff_output, (((1,), (1,)), ((), ())), preferred_element_type=jnp.float32
            )
            * scale_mid
        ).astype(jnp.bfloat16)
        dvalues = jnp.einsum(
            "hqk,nqhe->nkhe",
            attention,
            dmixed.reshape(sequences, positions, heads, head_size),
            preferred_element_type=jnp.float32,
        )
        dvalues = dvalues.astype(jnp.bfloat16).reshape(batch, inner_own)
        partial_value = jnp.dot(cols, eff_value, preferred_element_type=jnp.float32) * scale_in
        dvalues_all = lax.all_gather(dvalues, "fsdp", axis=1, tiled=True)
        values = lax.psum_scatter(
            partial_value.astype(jnp.bfloat16), "fsdp", scatter_dimension=1, tiled=True
        )
        mixed = jnp.einsum(
            "hqk,nkhe->nqhe",
            attention,
            values.reshape(sequences, positions, heads, head_size),
            preferred_element_type=jnp.float32,
        )
        mixed = mixed.astype(jnp.bfloat16).reshape(batch, inner_own)
        grad_value = contract_rows(cols, dvalues_all) * scale_in
        grad_output = contract_rows(mixed, cot) * scale_mid
        half_value = (value_num - learn_rate * grad_value) * 0.5
        half_output = (output_num - learn_rate * grad_output) * 0.5
        half_mass = push_mass * 0.5
        message = (
            half_value.astype(jnp.bfloat16),
            half_output.astype(jnp.bfloat16),
            half_mass.astype(jnp.bfloat16),
        )
        value_num, output_num, push_mass = half_value, half_output, half_mass
        if arrived is not None:
            value_num = value_num + arrived[0].astype(jnp.float32)
            output_num = output_num + arrived[1].astype(jnp.float32)
            push_mass = push_mass + arrived[2].astype(jnp.float32)
        arrived = jax.tree.map(lambda part: shifted(part, "group", distance), message)
    value_num = value_num + arrived[0].astype(jnp.float32)
    output_num = output_num + arrived[1].astype(jnp.float32)
    push_mass = push_mass + arrived[2].astype(jnp.float32)
    value_out = (value_num / push_mass[0]).astype(jnp.bfloat16)[None]
    output_out = (output_num / push_mass[0]).astype(jnp.bfloat16)[None]
    return (value_out, output_out, push_mass)


def on_device(
    inputs, cotangent, value_weight, output_weight, push_weight, position_bias, step_index
):
    head_count = position_bias.shape[0]
    own_heads = head_count // lax.axis_size("fsdp")
    bias = lax.dynamic_slice_in_dim(
        position_bias, lax.axis_index("fsdp") * own_heads, own_heads, axis=0
    )
    attention = jax.nn.softmax(bias, axis=-1).astype(jnp.bfloat16)
    value_num = value_weight[0].astype(jnp.float32)
    output_num = output_weight[0].astype(jnp.float32)
    columns = lax.all_to_all(inputs[0], "fsdp", split_axis=2, concat_axis=1, tiled=True)
    cot_all = lax.all_gather(cotangent[0], "fsdp", axis=1, tiled=True)
    branches = [functools.partial(run_window, first) for first in range(4)]
    return lax.switch(
        step_index[0] % 4,
        branches,
        columns,
        cot_all,
        attention,
        value_num,
        output_num,
        push_weight,
    )


def solution(mesh):
    placed = (
        P("group", None, "fsdp", None),
        P("group", None, "fsdp", None),
        P("group", "fsdp", None),
        P("group", "fsdp", None),
        P("group"),
        P(),
        P(),
    )
    return jax.shard_map(
        on_device,
        mesh=mesh,
        in_specs=placed,
        out_specs=(P("group", "fsdp", None), P("group", "fsdp", None), P("group")),
        check_vma=False,
    )
```

time: 1270 us -> 883 us (0.70)
  starting transfers between devices: 390 us -> 114 us
  blocking collectives: 53.6 us -> 0 us
  other arithmetic: 35.7 us -> 9.12 us
  matrix products: 87.1 us -> 66.4 us
    ppermute x12, starting transfers between devices: 352 us -> 106 us  [shifted(): return lax.ppermute(block, axis, route)]
    unnamed x16 -> x1, waiting for transfers between devices: 231 us -> 0.68 us
    reduce_scatter x0 -> x4, waiting for transfers between devices: none -> 169 us  [run_window(): lax.psum_scatter(partial_value.astype(jnp.bfloat16), 'fsdp', scatter_dime...]
    ppermute x12, waiting for transfers between devices: 55.4 us -> 115 us  [shifted(): return lax.ppermute(block, axis, route)]
    all_to_all x5 -> x0, blocking collectives: 53.6 us -> none  [the longest x3 31.6 us: on_device(): lax.all_to_all(dmixed_cols, 'fsdp', split_axis=0, concat_axis=1, tiled=True)]
    all_to_all x7 -> x1, starting transfers between devices: 37.8 us -> 7.4 us  [on_device(): lax.all_to_all(inputs[0], 'fsdp', split_axis=2, concat_axis=1, tiled=True)]
    unnamed x4 -> x0, loops' own time: 28.4 us -> none
    another operation x0 -> x1, loops' own time: none -> 22.6 us  [on_device(): lax.switch(step_index[0] % 4, branches, columns, cot_all, attention, valu...]
  transfers between devices with their start and end apart: 31 -> 22, of which waited for: 18 -> 12; matrix products, arithmetic and copies ran while one was open for 12% -> 13% of each run, Pallas kernels for 0% -> 0%
where the time goes in v1:
time: 883 us; the launch traced here: 873 us
  waiting for transfers between devices  586 us (66%)
  starting transfers between devices  114 us (13%)
  matrix products  66.4 us (8%)
  local copies, waits for them, and re-layouts  58.9 us (7%)
  loops' own time  22.6 us (3%)
  between operations  15.9 us (2%)
  other arithmetic  9.12 us (1%)
    all_gather x4, waiting for transfers between devices, run_window(): dvalues_all = lax.all_gather(dvalues, 'fsdp', axis=1, tiled=True)  212 us
    reduce_scatter x4, waiting for transfers between devices, run_window(): lax.psum_scatter(partial_value.astype(jnp.bfloat16), 'fsdp', scatter_dime...  169 us
    ppermute x12, waiting for transfers between devices, shifted(): return lax.ppermute(block, axis, route)  115 us
    ppermute x12, starting transfers between devices, shifted(): return lax.ppermute(block, axis, route)  106 us
    all_gather x1, waiting for transfers between devices, on_device(): cot_all = lax.all_gather(cotangent[0], 'fsdp', axis=1, tiled=True)  71.7 us
    dot_general x8, matrix products, contract_rows(): lax.dot_general(left, right, (((0,), (0,)), ((), ())), preferred_element_...  42.3 us
    unnamed x10, local copies, waits for them, and re-layouts  27.3 us
    another operation x1, loops' own time, on_device(): lax.switch(step_index[0] % 4, branches, columns, cot_all, attention, valu...  22.6 us
  transfers between devices with their start and end apart: 22, of which 12 were waited for; matrix products, arithmetic and copies ran while one was open for 13% of the time, Pallas kernels for 0%

profile of v1, /device:TPU:6, one launch (start us, length us, event | category | flops | bytes accessed | tf_op | source)
XLA Modules:
  0.0 872.8 jit_solution(9623351716998303573)
XLA Ops:
  7.9 6.1 copy.320
  14.0 5.3 bitcast_bitcast_fusion
  19.3 7.9 reshape.265
  27.2 7.4 all-to-all-start
  35.5 17.3 %all-to-all-done = bf16[8,2,32768]{2,1,0:T(2,128)(2,1)} async-done(((bf16[8,2,32768]{2,1,0:T(2,128)(2,1)}), bf16[8,2,32768]{2,1,0:T(2,128)(2,1)}, u32[]{:S(2)}, u32[]{:S(2)}) %all-to-all-start) | async-done | bytes 1048608 | tf_op jit(solution)/shard_map/all_to_all | solution.py:102
  52.8 7.0 reshape.266
  59.8 5.4 copy.383
  65.1 71.7 %all-gather.51.cloned.1.call-done = bf16[1,4,256,4096]{3,2,1,0:T(8,128)(2,1)} async-done(((bf16[1,4,32,4096]{3,2,1,0:T(8,128)(2,1)}), bf16[1,4,256,4096]{3,2,1,0:T(8,128)(2,1)}) %all-gather.51.cloned.1.call-update) | async-done | bytes 8388624 | tf_op jit(solution)/shard_map/all_gather | solution.py:103
  136.9 726.9 %conditional.1 = (bf16[1,256,4096]{2,1,0:T(8,128)(2,1)}, f32[1]{0:T(128)}, bf16[1,512,2048]{2,1,0:T(8,128)(2,1)}) conditional(s32[]{:T(128)} %clamp.3, (f32[1]{0:T(128)}, bf16[1,256,4096]{2,1,0:T(8,128)(2,1)}, bf16[4,256,4096]{2,1,0:T(8,128)(2,1)}, bf16[4,32,32]{2,1,0:T(8,128)(2,1)S(1)}, ...), branch_computations={%region_2.7_spmd, %region_7.12_spmd, %region_12.17_spmd, %region_1... | conditional | flops 8712617984 | bytes 437325024 | solution.py:105
  167.7 71.3 %reduce-scatter.41.cloned.1.call-done = bf16[256,256]{0,1:T(8,128)(2,1)} async-done(((bf16[256,2048]{0,1:T(8,128)(2,1)}), bf16[256,256]{0,1:T(8,128)(2,1)}) %reduce-scatter.41.cloned.1.call-update) | async-done | bytes 131088 | tf_op jit(solution)/shard_map/cond/branch_3_fun/reduce_scatter | solution.py:57
  251.0 43.2 %all-gather.43.cloned.1.call-done = bf16[256,2048]{1,0:T(8,128)(2,1)} async-done(((bf16[256,256]{1,0:T(8,128)(2,1)}), bf16[256,2048]{1,0:T(8,128)(2,1)}) %all-gather.43.cloned.1.call-update) | async-done | bytes 1048592 | tf_op jit(solution)/shard_map/cond/branch_3_fun/all_gather | solution.py:56
  302.0 87.3 %collective-permute-start.38 = (bf16[1]{0:T(256)(128)(2,1)}, bf16[1]{0:T(256)(128)(2,1)}, u32[]{:S(2)}, u32[]{:S(2)}) collective-permute-start(bf16[1]{0:T(256)(128)(2,1)} %convert_element_type.760), channel_id=1, source_target_pairs={{192,0},{200,8},{208,16},{216,24},{224,32},{232,40},{240,48},{248,... | collective-permute-start | bytes 14 | tf_op jit(solution)/shard_map/cond/branch_3_fun/ppermute | solution.py:16
  403.5 25.9 %reduce-scatter.43.cloned.1.call-done = bf16[256,256]{0,1:T(8,128)(2,1)} async-done(((bf16[256,2048]{0,1:T(8,128)(2,1)}), bf16[256,256]{0,1:T(8,128)(2,1)}) %reduce-scatter.43.cloned.1.call-update) | async-done | bytes 131088 | tf_op jit(solution)/shard_map/cond/branch_3_fun/reduce_scatter | solution.py:57
  431.2 5.0 fusion.492
  440.2 66.2 %collective-permute-done.41 = bf16[1]{0:T(256)(128)(2,1)} collective-permute-done((bf16[1]{0:T(256)(128)(2,1)}, bf16[1]{0:T(256)(128)(2,1)}, u32[]{:S(2)}, u32[]{:S(2)}) %collective-permute-start.41) | collective-permute-done | bytes 34 | tf_op jit(solution)/shard_map/cond/branch_3_fun/ppermute | solution.py:16
  513.8 5.9 fusion.494
  525.9 45.2 %all-gather.47.cloned.1.call-done = bf16[256,2048]{1,0:T(8,128)(2,1)} async-done(((bf16[256,256]{1,0:T(8,128)(2,1)}), bf16[256,2048]{1,0:T(8,128)(2,1)}) %all-gather.47.cloned.1.call-update) | async-done | bytes 1048592 | tf_op jit(solution)/shard_map/cond/branch_3_fun/all_gather | solution.py:56
  571.1 5.6 fusion.496
  585.4 124.1 %all-gather.49.cloned.1.call-done = bf16[256,2048]{1,0:T(8,128)(2,1)} async-done(((bf16[256,256]{1,0:T(8,128)(2,1)}), bf16[256,2048]{1,0:T(8,128)(2,1)}) %all-gather.49.cloned.1.call-update) | async-done | bytes 1048592 | tf_op jit(solution)/shard_map/cond/branch_3_fun/all_gather | solution.py:56
  709.5 6.9 fusion.495
  718.0 72.0 %reduce-scatter.47.cloned.1.call-done = bf16[256,256]{0,1:T(8,128)(2,1)} async-done(((bf16[256,2048]{0,1:T(8,128)(2,1)}), bf16[256,256]{0,1:T(8,128)(2,1)}) %reduce-scatter.47.cloned.1.call-update) | async-done | bytes 131088 | tf_op jit(solution)/shard_map/cond/branch_3_fun/reduce_scatter | solution.py:57
  791.8 6.7 fusion.493
  802.0 43.8 %collective-permute-done.44 = bf16[1]{0:T(256)(128)(2,1)} collective-permute-done((bf16[1]{0:T(256)(128)(2,1)}, bf16[1]{0:T(256)(128)(2,1)}, u32[]{:S(2)}, u32[]{:S(2)}) %collective-permute-start.44) | collective-permute-done | bytes 34 | tf_op jit(solution)/shard_map/cond/branch_3_fun/ppermute | solution.py:16
  856.7 5.7 fusion.373
  (126 shorter events, 91.3 us)
Async XLA Ops:
  7.2 129.7 %all-gather.51.cloned.1.call-start = ((), (), s32[]{:S(2)}) async-start(), calls=%async_computation.49 | async-start | bytes 9437184 | tf_op jit(solution)/shard_map/all_gather | solution.py:103
  27.2 25.6 %all-to-all-start = ((bf16[8,2,32768]{2,1,0:T(2,128)(2,1)}), bf16[8,2,32768]{2,1,0:T(2,128)(2,1)}, u32[]{:S(2)}, u32[]{:S(2)}) async-start(bf16[8,2,32768]{2,1,0:T(2,128)(2,1)} %reshape.265), calls=%async_computation.16 | async-start | bytes 2097152 | tf_op jit(solution)/shard_map/all_to_all | solution.py:102
  35.5 101.4 %copy-start.2 = (bf16[1,512,2048]{2,1,0:T(8,128)(2,1)S(1)}, bf16[1,512,2048]{2,1,0:T(8,128)(2,1)}, u32[]{:S(2)}) copy-start(bf16[1,512,2048]{2,1,0:T(8,128)(2,1)} %param.13) | copy-start | bytes 6291460
  153.9 85.1 %reduce-scatter.41.cloned.1.call-start = ((), (), s32[]{:S(2)}) async-start(), calls=%async_computation.42 | async-start | bytes 1179648 | tf_op jit(solution)/shard_map/cond/branch_3_fun/reduce_scatter | solution.py:57
  162.3 131.9 %all-gather.43.cloned.1.call-start = ((), (), s32[]{:S(2)}) async-start(), calls=%async_computation.41 | async-start | bytes 1179648 | tf_op jit(solution)/shard_map/cond/branch_3_fun/all_gather | solution.py:56
  167.0 227.7 %all-gather.45.cloned.1.call-start = ((), (), s32[]{:S(2)}) async-start(), calls=%async_computation.43 | async-start | bytes 1179648 | tf_op jit(solution)/shard_map/cond/branch_3_fun/all_gather | solution.py:56
  251.0 178.4 %reduce-scatter.43.cloned.1.call-start = ((), (), s32[]{:S(2)}) async-start(), calls=%async_computation.44 | async-start | bytes 1179648 | tf_op jit(solution)/shard_map/cond/branch_3_fun/reduce_scatter | solution.py:57
  297.7 101.7 %collective-permute-start.36 = (bf16[512,2048]{0,1:T(8,128)(2,1)}, bf16[512,2048]{0,1:T(8,128)(2,1)S(1)}, u32[]{:S(2)}, u32[]{:S(2)}) collective-permute-start(bf16[512,2048]{0,1:T(8,128)(2,1)} %get-tuple-element.270), channel_id=1, source_target_pairs={{192,0},{200,8},{208,16},{216,24},{224,32},{232,40},{240,48},{248,... | collective-permute-start | bytes 6291464 | tf_op jit(solution)/shard_map/cond/branch_3_fun/ppermute | solution.py:16
  302.0 210.0 %reduce-scatter.45.cloned.1.call-start = ((), (), s32[]{:S(2)}) async-start(), calls=%async_computation.46 | async-start | bytes 1179648 | tf_op jit(solution)/shard_map/cond/branch_3_fun/reduce_scatter | solution.py:57
  302.0 89.9 %collective-permute-start.38 = (bf16[1]{0:T(256)(128)(2,1)}, bf16[1]{0:T(256)(128)(2,1)}, u32[]{:S(2)}, u32[]{:S(2)}) collective-permute-start(bf16[1]{0:T(256)(128)(2,1)} %convert_element_type.760), channel_id=1, source_target_pairs={{192,0},{200,8},{208,16},{216,24},{224,32},{232,40},{240,48},{248,... | collective-permute-start | bytes 14 | tf_op jit(solution)/shard_map/cond/branch_3_fun/ppermute | solution.py:16
  392.6 114.5 %collective-permute-start.37 = (bf16[256,4096]{1,0:T(8,128)(2,1)}, bf16[256,4096]{1,0:T(8,128)(2,1)}, u32[]{:S(2)}, u32[]{:S(2)}) collective-permute-start(bf16[256,4096]{1,0:T(8,128)(2,1)} %get-tuple-element.268), channel_id=1, source_target_pairs={{192,0},{200,8},{208,16},{216,24},{224,32},{232,40},{240,48},{248,... | collective-permute-start | bytes 6291464 | tf_op jit(solution)/shard_map/cond/branch_3_fun/ppermute | solution.py:16
  403.2 167.8 %all-gather.47.cloned.1.call-start = ((), (), s32[]{:S(2)}) async-start(), calls=%async_computation.45 | async-start | bytes 1179648 | tf_op jit(solution)/shard_map/cond/branch_3_fun/all_gather | solution.py:56
  436.3 70.8 %copy-start.14 = (f32[256,4096]{1,0:T(8,128)}, f32[256,4096]{1,0:T(8,128)S(1)}, u32[]{:S(2)}) copy-start(f32[256,4096]{1,0:T(8,128)S(1)} %get-tuple-element.275) | copy-start | bytes 12582916 | tf_op jit(solution)/shard_map/cond
  436.3 83.5 %collective-permute-start.40 = (bf16[256,4096]{1,0:T(8,128)(2,1)}, bf16[256,4096]{1,0:T(8,128)(2,1)S(1)}, u32[]{:S(2)}, u32[]{:S(2)}) collective-permute-start(bf16[256,4096]{1,0:T(8,128)(2,1)} %get-tuple-element.274), channel_id=1, source_target_pairs={{248,0},{0,8},{8,16},{16,24},{24,32},{32,40},{40,48},{48,56},{56,6... | collective-permute-start | bytes 6291464 | tf_op jit(solution)/shard_map/cond/branch_3_fun/ppermute | solution.py:16
  436.3 70.2 %collective-permute-start.41 = (bf16[1]{0:T(256)(128)(2,1)}, bf16[1]{0:T(256)(128)(2,1)}, u32[]{:S(2)}, u32[]{:S(2)}) collective-permute-start(bf16[1]{0:T(256)(128)(2,1)} %convert_element_type.776), channel_id=1, source_target_pairs={{248,0},{0,8},{8,16},{16,24},{24,32},{32,40},{40,48},{48,56},{56,6... | collective-permute-start | bytes 14 | tf_op jit(solution)/shard_map/cond/branch_3_fun/ppermute | solution.py:16
  507.0 69.7 %collective-permute-start.39 = (bf16[512,2048]{0,1:T(8,128)(2,1)}, bf16[512,2048]{0,1:T(8,128)(2,1)}, u32[]{:S(2)}, u32[]{:S(2)}) collective-permute-start(bf16[512,2048]{0,1:T(8,128)(2,1)} %get-tuple-element.272), channel_id=1, source_target_pairs={{248,0},{0,8},{8,16},{16,24},{24,32},{32,40},{40,48},{48,56},{56,6... | collective-permute-start | bytes 6291464 | tf_op jit(solution)/shard_map/cond/branch_3_fun/ppermute | solution.py:16
  511.9 197.6 %all-gather.49.cloned.1.call-start = ((), (), s32[]{:S(2)}) async-start(), calls=%async_computation.47 | async-start | bytes 1179648 | tf_op jit(solution)/shard_map/cond/branch_3_fun/all_gather | solution.py:56
  525.9 264.1 %reduce-scatter.47.cloned.1.call-start = ((), (), s32[]{:S(2)}) async-start(), calls=%async_computation.48 | async-start | bytes 1179648 | tf_op jit(solution)/shard_map/cond/branch_3_fun/reduce_scatter | solution.py:57
  582.2 269.0 %collective-permute-start.42 = (bf16[512,2048]{0,1:T(8,128)(2,1)}, bf16[512,2048]{0,1:T(8,128)(2,1)}, u32[]{:S(2)}, u32[]{:S(2)}) collective-permute-start(bf16[512,2048]{0,1:T(8,128)(2,1)} %get-tuple-element.282), channel_id=1, source_target_pairs={{240,0},{248,8},{0,16},{8,24},{16,32},{24,40},{32,48},{40,56},{48,... | collective-permute-start | bytes 6291464 | tf_op jit(solution)/shard_map/cond/branch_3_fun/ppermute | solution.py:16
  582.8 273.9 %collective-permute-start.46 = (bf16[256,4096]{1,0:T(8,128)(2,1)}, bf16[256,4096]{1,0:T(8,128)(2,1)}, u32[]{:S(2)}, u32[]{:S(2)}) collective-permute-start(bf16[256,4096]{1,0:T(8,128)(2,1)} %get-tuple-element.278), channel_id=1, source_target_pairs={{240,0},{248,8},{0,16},{8,24},{16,32},{24,40},{32,48},{40,56},{48,... | collective-permute-start | bytes 6291464 | tf_op jit(solution)/shard_map/cond/branch_3_fun/ppermute | solution.py:16
  716.4 134.7 %collective-permute-start.43 = (bf16[512,2048]{0,1:T(8,128)(2,1)}, bf16[512,2048]{0,1:T(8,128)(2,1)}, u32[]{:S(2)}, u32[]{:S(2)}) collective-permute-start(bf16[512,2048]{0,1:T(8,128)(2,1)} %get-tuple-element.280), channel_id=1, source_target_pairs={{224,0},{232,8},{240,16},{248,24},{0,32},{8,40},{16,48},{24,56},{3... | collective-permute-start | bytes 6291464 | tf_op jit(solution)/shard_map/cond/branch_3_fun/ppermute | solution.py:16
  798.5 58.2 %collective-permute-start.47 = (bf16[256,4096]{1,0:T(8,128)(2,1)}, bf16[256,4096]{1,0:T(8,128)(2,1)}, u32[]{:S(2)}, u32[]{:S(2)}) collective-permute-start(bf16[256,4096]{1,0:T(8,128)(2,1)} %get-tuple-element.276), channel_id=1, source_target_pairs={{224,0},{232,8},{240,16},{248,24},{0,32},{8,40},{16,48},{24,56},{3... | collective-permute-start | bytes 6291464 | tf_op jit(solution)/shard_map/cond/branch_3_fun/ppermute | solution.py:16
  800.1 45.7 %collective-permute-start.44 = (bf16[1]{0:T(256)(128)(2,1)}, bf16[1]{0:T(256)(128)(2,1)}, u32[]{:S(2)}, u32[]{:S(2)}) collective-permute-start(bf16[1]{0:T(256)(128)(2,1)} %convert_element_type.787), channel_id=1, source_target_pairs={{240,0},{248,8},{0,16},{8,24},{16,32},{24,40},{32,48},{40,56},{48,... | collective-permute-start | bytes 14 | tf_op jit(solution)/shard_map/cond/branch_3_fun/ppermute | solution.py:16
  845.8 4.7 collective-permute-start.45
  (12 other events, 161.3 us)
Sparse Core Ops, SparseCore 0:
  10.6 126.1 all-gather.50
  162.4 76.5 reduce-scatter.40
  241.8 52.3 all-gather.42
  296.8 52.1 all-gather.44
  353.3 76.0 reduce-scatter.42
  433.2 77.2 reduce-scatter.44
  513.3 57.7 all-gather.46
  573.8 135.6 all-gather.48
  714.0 75.9 reduce-scatter.46

commit v2 on v1

v2 whole, which is shorter than its diff:
```python
import functools
import math

import jax
import jax.numpy as jnp
from jax import lax
from jax.experimental import pallas as pl
from jax.experimental.pallas import tpu as pltpu
from jax.sharding import PartitionSpec as P

DISTANCES = (1, 2, 4, 8)
MESH = pl.DeviceIdType.MESH
F32 = jnp.float32
BF16 = jnp.bfloat16


def window_kernel(
    first,
    sizes,
    inputs,
    cotangent,
    value_in,
    output_in,
    mass_in,
    bias,
    value_out,
    output_out,
    mass_out,
    x_cols,
    x_turned,
    cot_all,
    value_w,
    output_w,
    value_msg,
    output_msg,
    mass_msg,
    value_got,
    output_got,
    mass_got,
    part,
    part_got,
    dvalues_all,
    mix,
    mix_turned,
    mixed_turned,
    total,
    inverse,
    load_sem,
    own_sem,
    x_send,
    x_recv,
    cot_send,
    cot_recv,
    part_send,
    part_recv,
    dv_send,
    dv_recv,
    value_send,
    value_recv,
    output_send,
    output_recv,
    mass_send,
    mass_recv,
):
    groups, peers, steps, positions, heads, head_size = sizes
    batch = peers * positions
    v_cols = value_w.shape[2]
    o_cols = output_w.shape[2]
    x_width = x_cols.shape[3]
    scale_in = 1.0 / math.sqrt(x_width * peers)
    scale_mid = 1.0 / math.sqrt(v_cols * peers)
    g = lax.axis_index("group")
    f = lax.axis_index("fsdp")

    def peer(k):
        return lax.rem(f + k, peers)

    def ahead(distance):
        return lax.rem(g + distance, groups)

    def behind(distance):
        return lax.rem(g + groups - distance, groups)

    def remote(src, dst, send, recv, device):
        return pltpu.make_async_remote_copy(
            src_ref=src,
            dst_ref=dst,
            send_sem=send,
            recv_sem=recv,
            device_id=device,
            device_id_type=MESH,
        )

    def loads():
        for c in range(peers):
            yield pltpu.make_async_copy(
                value_in.at[0, :, pl.ds(c * v_cols, v_cols)], value_msg.at[1, c], load_sem.at[0, c]
            )
            yield pltpu.make_async_copy(
                output_in.at[0, :, pl.ds(c * o_cols, o_cols)],
                output_msg.at[1, c],
                load_sem.at[1, c],
            )

    def columns_of(p):
        return pl.ds(pl.multiple_of(p * x_width, x_width), x_width)

    own_x = pltpu.make_async_copy(
        inputs.at[0, :, :, columns_of(f)], x_cols.at[:, f], own_sem.at[0]
    )
    own_cot = pltpu.make_async_copy(cotangent.at[0], cot_all.at[:, f], own_sem.at[1])

    def x_copy(late, k):
        when = pl.ds(1, steps - 1) if late else pl.ds(0, 1)
        return remote(
            inputs.at[0, when, :, columns_of(peer(k))],
            x_cols.at[when, f],
            x_send.at[late, k],
            x_recv.at[late, k],
            (g, peer(k)),
        )

    def cot_copy(t, k):
        return remote(
            cotangent.at[0, t],
            cot_all.at[t, f],
            cot_send.at[t, k],
            cot_recv.at[t, k],
            (g, peer(k)),
        )

    def part_copy(t, k):
        return remote(
            part.at[k],
            part_got.at[t, k],
            part_send.at[t, k],
            part_recv.at[t, k],
            (g, peer(k)),
        )

    def dv_copy(t, k):
        return remote(
            dvalues_all.at[t, f],
            dvalues_all.at[t, f],
            dv_send.at[t, k],
            dv_recv.at[t, k],
            (g, peer(k)),
        )

    def target(t):
        return (ahead(DISTANCES[(first + t) % 4]), f)

    def value_copy(t, c):
        return remote(
            value_msg.at[t % 2, c],
            value_got.at[t, c],
            value_send.at[t, c],
            value_recv.at[t, c],
            target(t),
        )

    def output_copy(t, c):
        return remote(
            output_msg.at[t % 2, c],
            output_got.at[t, c],
            output_send.at[t, c],
            output_recv.at[t, c],
            target(t),
        )

    def mass_copy(t):
        return remote(
            mass_msg.at[t], mass_got.at[t], mass_send.at[t], mass_recv.at[t], target(t)
        )

    def each(body, start=0, stop=peers):
        def run(i, carry):
            body(i)
            return carry

        lax.fori_loop(start, stop, run, 0)

    for copy in loads():
        copy.start()
    own_x.start()
    own_cot.start()

    barrier = pltpu.get_barrier_semaphore()
    for k in range(1, peers):
        pl.semaphore_signal(barrier, inc=1, device_id=(g, peer(k)), device_id_type=MESH)
    for distance in DISTANCES:
        pl.semaphore_signal(barrier, inc=1, device_id=(behind(distance), f), device_id_type=MESH)
    pl.semaphore_wait(barrier, peers - 1 + len(DISTANCES))

    each(lambda k: x_copy(0, k).start(), 1)
    each(lambda k: cot_copy(0, k).start(), 1)
    each(lambda k: x_copy(1, k).start(), 1)

    for copy in loads():
        copy.wait()

    def widen(c):
        value_w[c] = value_msg[1, c].astype(F32)
        output_w[c] = output_msg[1, c].astype(F32)

    each(widen)

    spread = (
        lax.rem(lax.broadcasted_iota(jnp.int32, (batch, positions), 0), positions)
        == lax.broadcasted_iota(jnp.int32, (batch, positions), 1)
    ).astype(BF16)
    same = (
        lax.broadcasted_iota(jnp.int32, (batch, batch), 0) // positions
        == lax.broadcasted_iota(jnp.int32, (batch, batch), 1) // positions
    )
    for h in range(heads):
        logits = bias[f * heads + h]
        weights = jnp.exp(logits - jnp.max(logits, axis=-1, keepdims=True))
        weights = (weights / jnp.sum(weights, axis=-1, keepdims=True)).astype(BF16)
        for held, dims in ((mix, ((1,), (0,))), (mix_turned, ((1,), (1,)))):
            tall = lax.dot_general(spread, weights, (dims, ((), ())), preferred_element_type=F32)
            wide = lax.dot_general(
                tall.astype(BF16), spread, (((1,), (1,)), ((), ())), preferred_element_type=F32
            )
            held[h] = jnp.where(same, wide, 0.0).astype(BF16)

    head_of = lax.broadcasted_iota(jnp.int32, (batch, v_cols), 1) // head_size

    def by_heads(weights, block):
        result = jnp.zeros((batch, v_cols), F32)
        for h in range(heads):
            product = jnp.dot(weights[h], block, preferred_element_type=F32)
            result = jnp.where(head_of == h, product, result)
        return result.astype(BF16)

    mass = mass_in[...]
    own_x.wait()
    own_cot.wait()
    each(lambda k: x_copy(0, k).wait_recv(), 1)

    for t in range(steps):
        slot = t % 2
        inverse[...] = 1.0 / mass

        if t == 1:
            each(lambda k: x_copy(1, k).wait_recv(), 1)
        x_turned[...] = x_cols[t].reshape(batch, x_width).T

        def values_of(k, t=t):
            c = peer(k)
            if t >= 2:
                value_copy(t - 2, c).wait_recv()
                value_w[c] = value_w[c] + value_got[t - 2, c].astype(F32)
            effective = (value_w[c] * inverse[0:1, 0:v_cols]).astype(BF16)
            product = jnp.dot(
                x_cols[t].reshape(batch, x_width), effective, preferred_element_type=F32
            )
            return (product * scale_in).astype(BF16)

        def send_part(k, t=t, values_of=values_of):
            part[k] = values_of(k)
            part_copy(t, k).start()

        def forward(t=t, values_of=values_of, send_part=send_part):
            each(send_part, 1)
            part_got[t, 0] = values_of(0)

        def add_dmixed(c, t=t):
            if t >= 2:
                output_copy(t - 2, c).wait_recv()
                output_w[c] = output_w[c] + output_got[t - 2, c].astype(F32)
            effective = (output_w[c] * inverse[0:1, 0:o_cols]).astype(BF16)
            cot = cot_all[t, :, :, pl.ds(pl.multiple_of(c * o_cols, o_cols), o_cols)]
            total[...] += lax.dot_general(
                cot.reshape(batch, o_cols),
                effective,
                (((1,), (1,)), ((), ())),
                preferred_element_type=F32,
            )

        def backward(t=t, add_dmixed=add_dmixed):
            each(lambda k: cot_copy(t, k).wait_recv(), 1)
            total[...] = jnp.zeros_like(total)
            each(add_dmixed)
            dmixed = (total[...] * scale_mid).astype(BF16)
            dvalues_all[t, f] = by_heads(mix_turned, dmixed)
            each(lambda k: dv_copy(t, k).start(), 1)

        def update_output(c, t=t, slot=slot):
            cot = cot_all[t, :, :, pl.ds(pl.multiple_of(c * o_cols, o_cols), o_cols)]
            grad = jnp.dot(
                mixed_turned[...], cot.reshape(batch, o_cols), preferred_element_type=F32
            )
            half = 0.5 * output_w[c] - (0.25 * scale_mid) * grad
            output_w[c] = half
            if t >= 2:
                output_copy(t - 2, c).wait_send()
            output_msg[slot, c] = half.astype(BF16)
            output_copy(t, c).start()

        def outputs(t=t, update_output=update_output):
            each(lambda k: part_copy(t, k).wait(), 1)
            summed = part_got[t, 0].astype(F32)
            for k in range(1, peers):
                summed = summed + part_got[t, k].astype(F32)
            mixed_turned[...] = by_heads(mix, summed.astype(BF16)).T
            each(update_output)

        def update_value(j, t=t, slot=slot):
            c = peer(j)
            grad = jnp.dot(x_turned[...], dvalues_all[t, c], preferred_element_type=F32)
            half = 0.5 * value_w[c] - (0.25 * scale_in) * grad
            value_w[c] = half
            if t >= 2:
                value_copy(t - 2, c).wait_send()
            value_msg[slot, c] = half.astype(BF16)
            value_copy(t, c).start()

        def update_other(j, t=t, update_value=update_value):
            dv_copy(t, peers - j).wait_recv()
            update_value(j)

        def values(t=t, update_value=update_value, update_other=update_other):
            each(update_other, 1)
            update_value(0)

        half_mass = mass * 0.5
        if t < 2:
            forward()
            backward()
        else:
            backward()
            forward()
        if t + 1 < steps:
            each(lambda k: cot_copy(t + 1, k).start(), 1)
        if t < 2:
            outputs()
            values()
        else:
            values()
            outputs()
        mass_msg[t] = half_mass.astype(BF16)
        mass_copy(t).start()
        mass = half_mass
        if t >= 1:
            mass_copy(t - 1).wait_recv()
            mass = mass + mass_got[t - 1].astype(F32)

    last = steps - 1
    mass_copy(last).wait_recv()
    mass = mass + mass_got[last].astype(F32)
    mass_out[...] = mass
    inverse[...] = 1.0 / mass

    def value_store(c):
        return pltpu.make_async_copy(
            value_msg.at[0, c],
            value_out.at[0, :, pl.ds(pl.multiple_of(c * v_cols, v_cols), v_cols)],
            load_sem.at[0, c],
        )

    def output_store(c):
        return pltpu.make_async_copy(
            output_msg.at[0, c],
            output_out.at[0, :, pl.ds(pl.multiple_of(c * o_cols, o_cols), o_cols)],
            load_sem.at[1, c],
        )

    def finish_value(j):
        c = peer(j)
        value_copy(last - 1, c).wait()
        value_copy(last, c).wait_recv()
        result = (
            value_w[c] + value_got[last - 1, c].astype(F32) + value_got[last, c].astype(F32)
        )
        value_msg[0, c] = (result * inverse[0:1, 0:v_cols]).astype(BF16)
        value_store(c).start()

    def finish_output(c):
        output_copy(last - 1, c).wait()
        output_copy(last, c).wait_recv()
        result = (
            output_w[c] + output_got[last - 1, c].astype(F32) + output_got[last, c].astype(F32)
        )
        output_msg[0, c] = (result * inverse[0:1, 0:o_cols]).astype(BF16)
        output_store(c).start()

    each(finish_value, 1)
    finish_value(0)
    each(finish_output)

    def settle(k):
        x_copy(0, k).wait_send()
        x_copy(1, k).wait_send()
        for t in range(steps):
            cot_copy(t, k).wait_send()
            dv_copy(t, k).wait_send()

    each(settle, 1)

    def settle_chunk(c):
        value_copy(last, c).wait_send()
        output_copy(last, c).wait_send()
        value_store(c).wait()
        output_store(c).wait()

    each(settle_chunk)
    for t in range(steps):
        mass_copy(t).wait_send()


def run_window(first, inputs, cotangent, value_weight, output_weight, mass, bias):
    groups = lax.axis_size("group")
    peers = lax.axis_size("fsdp")
    _, steps, positions, width = inputs.shape
    rows, inner = value_weight.shape[1:]
    own_inner = output_weight.shape[1]
    heads = bias.shape[0] // peers
    head_size = own_inner // heads
    batch = positions * peers
    o_cols = width // peers
    lanes = mass.shape[1]
    dma = pltpu.SemaphoreType.DMA
    hbm = pl.BlockSpec(memory_space=pl.ANY)
    vmem = pl.BlockSpec(memory_space=pltpu.VMEM)
    sizes = (groups, peers, steps, positions, heads, head_size)
    return pl.pallas_call(
        functools.partial(window_kernel, first, sizes),
        out_shape=(
            jax.ShapeDtypeStruct(value_weight.shape, BF16),
            jax.ShapeDtypeStruct(output_weight.shape, BF16),
            jax.ShapeDtypeStruct(mass.shape, F32),
        ),
        in_specs=[hbm, hbm, hbm, hbm, vmem, vmem],
        out_specs=(hbm, hbm, vmem),
        scratch_shapes=[
            pltpu.VMEM((steps, peers, positions, rows), BF16),
            pltpu.VMEM((rows, batch), BF16),
            pltpu.VMEM((steps, peers, positions, width), BF16),
            pltpu.VMEM((peers, rows, own_inner), F32),
            pltpu.VMEM((peers, own_inner, o_cols), F32),
            pltpu.VMEM((2, peers, rows, own_inner), BF16),
            pltpu.VMEM((2, peers, own_inner, o_cols), BF16),
            pltpu.VMEM((steps, *mass.shape), BF16),
            pltpu.VMEM((steps, peers, rows, own_inner), BF16),
            pltpu.VMEM((steps, peers, own_inner, o_cols), BF16),
            pltpu.VMEM((steps, *mass.shape), BF16),
            pltpu.VMEM((peers, batch, own_inner), BF16),
            pltpu.VMEM((steps, peers, batch, own_inner), BF16),
            pltpu.VMEM((steps, peers, batch, own_inner), BF16),
            pltpu.VMEM((heads, batch, batch), BF16),
            pltpu.VMEM((heads, batch, batch), BF16),
            pltpu.VMEM((own_inner, batch), BF16),
            pltpu.VMEM((batch, own_inner), F32),
            pltpu.VMEM(mass.shape, F32),
            dma((2, peers)),
            dma((2,)),
            dma((2, peers)),
            dma((2, peers)),
            dma((steps, peers)),
            dma((steps, peers)),
            dma((steps, peers)),
            dma((steps, peers)),
            dma((steps, peers)),
            dma((steps, peers)),
            dma((steps, peers)),
            dma((steps, peers)),
            dma((steps, peers)),
            dma((steps, peers)),
            dma((steps,)),
            dma((steps,)),
        ],
        compiler_params=pltpu.CompilerParams(
            collective_id=first, has_side_effects=True, vmem_limit_bytes=63 << 20
        ),
        name="window",
    )(inputs, cotangent, value_weight, output_weight, mass, bias)


def on_device(
    inputs, cotangent, value_weight, output_weight, push_weight, position_bias, step_index
):
    mass = jnp.broadcast_to(push_weight[:, None], (16, 512))
    value_out, output_out, mass = lax.switch(
        step_index[0] % 4,
        [functools.partial(run_window, first) for first in range(4)],
        inputs,
        cotangent,
        value_weight,
        output_weight,
        mass,
        position_bias,
    )
    return (value_out, output_out, mass[0, :1])


def solution(mesh):
    placed = (
        P("group", None, "fsdp", None),
        P("group", None, "fsdp", None),
        P("group", "fsdp", None),
        P("group", "fsdp", None),
        P("group"),
        P(),
        P(),
    )
    return jax.shard_map(
        on_device,
        mesh=mesh,
        in_specs=placed,
        out_specs=(P("group", "fsdp", None), P("group", "fsdp", None), P("group")),
        check_vma=False,
    )
```

time: 883 us -> 597 us (0.68)
  the two profiles are of different devices: /device:TPU:6 before, /device:TPU:26 now
where the time goes in v2:
time: 597 us
  Pallas kernels  589 us (99%)
    pallas_call x1, Pallas kernels, run_window(): pl.pallas_call(functools.partial(window_kernel, first, sizes), out_shape=...  589 us

profile of v2, /device:TPU:26, one launch (start us, length us, event | category | flops | bytes accessed | tf_op | source)
XLA Modules:
  0.0 597.3 jit_solution(11943072429791836308)
XLA Ops:
  2.0 590.7 %conditional.1 = (bf16[1,512,2048]{2,1,0:T(8,128)(2,1)}, bf16[1,256,4096]{2,1,0:T(8,128)(2,1)}, f32[1]{0:T(128)}) conditional(s32[]{:T(128)} %clamp.3, (bf16[1,4,32,4096]{3,2,1,0:T(8,128)(2,1)}, bf16[1,4,32,4096]{3,2,1,0:T(8,128)(2,1)}, bf16[1,512,2048]{2,1,0:T(8,128)(2,1)}, bf16[1,256,4096]{2,1,0:T(8,128)(2,1)}, ...), branch_computations={%region_0.1_spmd, %region_1.2_spmd, %region_2.3_spmd, %region_3.4_... | conditional | bytes 32 | solution.py:484
  2.5 588.9 %window.7 = (bf16[1,512,2048]{2,1,0:T(8,128)(2,1)}, bf16[1,256,4096]{2,1,0:T(8,128)(2,1)}, f32[16,512]{1,0:T(8,128)}) custom-call(bf16[1,4,32,4096]{3,2,1,0:T(8,128)(2,1)} %get-tuple-element.88.inputs, bf16[1,4,32,4096]{3,2,1,0:T(8,128)(2,1)} %get-tuple-element.89.cotangent, bf16[1,512,2048]{2,1,0:T(8,128)(2,1)} %get-tuple-element.90.value_in, ...), custom_call_target="tpu_custom_call" | custom-call | tf_op jit(solution)/shard_map/cond/branch_3_fun/window/pallas_call | solution.py:427
  591.4 1.2 slice.12
  592.6 0.0 copy-start
  592.6 3.3 copy.30
  595.9 0.0 copy-done
  595.9 1.3 copy.31
  (1 shorter events, 0.0 us)
Async XLA Ops:
  592.6 3.3 copy-start

commit v3 on v2

--- a/solution.py
+++ b/solution.py
@@ -9,6 +9,10 @@
 from jax.sharding import PartitionSpec as P
 
 DISTANCES = (1, 2, 4, 8)
+RELAY = 12
+SIDE = 8
+PACE = ((4, 6), (2, 3), (16, 16), (16, 16))
+DETOUR = ((4, 4), (4, 4), (4, 4), (4, 4))
 MESH = pl.DeviceIdType.MESH
 F32 = jnp.float32
 BF16 = jnp.bfloat16
@@ -39,6 +43,11 @@
     mass_got,
     part,
     part_got,
+    across,
+    across_got,
+    relay,
+    side_one,
+    side_two,
     dvalues_all,
     mix,
     mix_turned,
@@ -61,6 +70,12 @@
     output_recv,
     mass_send,
     mass_recv,
+    across_send,
+    across_recv,
+    relay_send,
+    relay_recv,
+    side_send,
+    side_recv,
 ):
     groups, peers, steps, positions, heads, head_size = sizes
     batch = peers * positions
@@ -71,9 +86,21 @@
     scale_mid = 1.0 / math.sqrt(v_cols * peers)
     g = lax.axis_index("group")
     f = lax.axis_index("fsdp")
+    row = peers // 2
+    y_half = f // row
+    x_place = lax.rem(f, row)
+    slow_step = (3 - first) % steps
+    detour = DETOUR[first][0] + (DETOUR[first][1] - DETOUR[first][0]) * lax.rem(g // 2, 2)
+    values_lead = slow_step >= 2
 
     def peer(k):
         return lax.rem(f + k, peers)
+
+    def beside(j, s=0):
+        return lax.rem(y_half + s, 2) * row + lax.rem(x_place + j, row)
+
+    def chunk_at(p):
+        return beside(lax.rem(p // 2 + 1, row), lax.rem(p, 2))
 
     def ahead(distance):
         return lax.rem(g + distance, groups)
@@ -121,30 +148,53 @@
         )
 
     def cot_copy(t, k):
-        return remote(
-            cotangent.at[0, t],
-            cot_all.at[t, f],
+        block = beside(0, k // row)
+        to = beside(lax.rem(k, row)) if not isinstance(k, int) else beside(0, 1)
+        return remote(
+            cot_all.at[t, block],
+            cot_all.at[t, block],
             cot_send.at[t, k],
             cot_recv.at[t, k],
-            (g, peer(k)),
-        )
-
-    def part_copy(t, k):
-        return remote(
-            part.at[k],
-            part_got.at[t, k],
-            part_send.at[t, k],
-            part_recv.at[t, k],
-            (g, peer(k)),
-        )
+            (g, to),
+        )
+
+    def cot_first(t, k):
+        to = beside(k) if not isinstance(k, int) else beside(0, 1)
+        return remote(
+            cotangent.at[0, t], cot_all.at[t, f], cot_send.at[t, k], cot_recv.at[t, k], (g, to)
+        )
+
+    def cot_lead(t):
+        cot_first(t, 0).start()
+        each(lambda j: cot_first(t, j).start(), 1, row)
+
+    def cot_pass(t):
+        cot_copy(t, 0).wait_recv()
+        each(lambda j: cot_copy(t, row + j).start(), 1, row)
 
     def dv_copy(t, k):
-        return remote(
-            dvalues_all.at[t, f],
-            dvalues_all.at[t, f],
+        block = beside(0, k // row)
+        to = beside(lax.rem(k, row)) if not isinstance(k, int) else beside(0, 1)
+        return remote(
+            dvalues_all.at[t, block],
+            dvalues_all.at[t, block],
             dv_send.at[t, k],
             dv_recv.at[t, k],
-            (g, peer(k)),
+            (g, to),
+        )
+
+    def part_copy(t, j):
+        return remote(
+            part.at[j],
+            part_got.at[t, j],
+            part_send.at[t, j],
+            part_recv.at[t, j],
+            (g, beside(j)),
+        )
+
+    def across_copy(t):
+        return remote(
+            across, across_got.at[t], across_send.at[t], across_recv.at[t], (g, beside(0, 1))
         )
 
     def target(t):
@@ -168,6 +218,131 @@
             target(t),
         )
 
+    def into_relay(p):
+        c = chunk_at(p) if values_lead else p
+        held, sent = (value_msg, value_send) if values_lead else (output_msg, output_send)
+        return remote(
+            held.at[slow_step % 2, c],
+            relay.at[p],
+            sent.at[slow_step, c],
+            relay_recv.at[p],
+            (behind(RELAY), f),
+        )
+
+    def from_relay(p):
+        c = chunk_at(p) if values_lead else p
+        got, landed = (value_got, value_recv) if values_lead else (output_got, output_recv)
+        return remote(
+            relay.at[p],
+            got.at[slow_step, c],
+            relay_send.at[p],
+            landed.at[slow_step, c],
+            (behind(RELAY), f),
+        )
+
+    def side_step(i):
+        return (i - first) % steps
+
+    def goes_aside(i):
+        return lax.rem(g, 4) >= 3 - i
+
+    def into_side(i, p):
+        t = side_step(i)
+        values = t >= 2
+        c = chunk_at(p) if values else p
+        held, sent = (value_msg, value_send) if values else (output_msg, output_send)
+        return remote(
+            held.at[t % 2, c],
+            (side_one, side_two)[i].at[p],
+            sent.at[t, c],
+            side_recv.at[i, p],
+            (behind(3 - i), f),
+        )
+
+    def from_side(i, p):
+        t = side_step(i)
+        values = t >= 2
+        c = chunk_at(p) if values else p
+        got, landed = (value_got, value_recv) if values else (output_got, output_recv)
+        return remote(
+            (side_one, side_two)[i].at[p],
+            got.at[t, c],
+            side_send.at[i, p],
+            landed.at[t, c],
+            (ahead(4), f),
+        )
+
+    def at_side(i, body):
+        @pl.when(lax.rem(g, 4) <= i)
+        def _():
+            each(body, 0, SIDE)
+
+    def pass_side(i):
+        def one(p):
+            into_side(i, p).wait_recv()
+            from_side(i, p).start()
+
+        at_side(i, one)
+
+    def pass_relay():
+        def one(p):
+            into_relay(p).wait_recv()
+            from_relay(p).start()
+
+        each(one, 0, detour)
+
+    def send_message(t, copy, values, p):
+        if t == slow_step and values == values_lead:
+
+            @pl.when(p < detour)
+            def _():
+                into_relay(p).start()
+
+            @pl.when(p >= detour)
+            def _():
+                copy.start()
+
+        elif (first + t) % 4 < 2 and values == (t >= 2):
+            i = (first + t) % 4
+            aside = jnp.logical_and(goes_aside(i), p < SIDE)
+
+            @pl.when(aside)
+            def _():
+                into_side(i, p).start()
+
+            @pl.when(jnp.logical_not(aside))
+            def _():
+                copy.start()
+
+        else:
+            copy.start()
+
+    def span(t, values, point):
+        marks = PACE[(first + t) % 4] if t + 1 < steps else (2 * peers, 2 * peers)
+        marks = (0, *marks, 2 * peers)
+        shift = 0 if values == (t >= 2) else peers
+        return tuple(min(max(m - shift, 0), peers) for m in marks[point : point + 2])
+
+    def send_value(t, p):
+        send_message(t, value_copy(t, chunk_at(p)), True, p)
+
+    def send_output(t, p):
+        send_message(t, output_copy(t, p), False, p)
+
+    def send_later(t, point):
+        each(lambda p: send_output(t, p), *span(t, False, point))
+        each(lambda p: send_value(t, p), *span(t, True, point))
+
+    def send_prompt(t, values, p):
+        send = send_value if values else send_output
+        if span(t, values, 0)[1] == peers:
+            send(t, p)
+        elif span(t, values, 0)[1] > 0:
+
+            @pl.when(p < span(t, values, 0)[1])
+            def _():
+                send(t, p)
+
     def mass_copy(t):
         return remote(
             mass_msg.at[t], mass_got.at[t], mass_send.at[t], mass_recv.at[t], target(t)
@@ -190,10 +365,13 @@
         pl.semaphore_signal(barrier, inc=1, device_id=(g, peer(k)), device_id_type=MESH)
     for distance in DISTANCES:
         pl.semaphore_signal(barrier, inc=1, device_id=(behind(distance), f), device_id_type=MESH)
-    pl.semaphore_wait(barrier, peers - 1 + len(DISTANCES))
+    pl.semaphore_signal(barrier, inc=1, device_id=(ahead(RELAY), f), device_id_type=MESH)
+    for distance in (2, 3):
+        pl.semaphore_signal(barrier, inc=1, device_id=(ahead(distance), f), device_id_type=MESH)
+    pl.semaphore_wait(barrier, peers + len(DISTANCES) + 2)
 
     each(lambda k: x_copy(0, k).start(), 1)
-    each(lambda k: cot_copy(0, k).start(), 1)
+    cot_lead(0)
     each(lambda k: x_copy(1, k).start(), 1)
 
     for copy in loads():
@@ -204,6 +382,7 @@
         output_w[c] = output_msg[1, c].astype(F32)
 
     each(widen)
+    cot_pass(0)
 
     spread = (
         lax.rem(lax.broadcasted_iota(jnp.int32, (batch, positions), 0), positions)
@@ -246,8 +425,8 @@
             each(lambda k: x_copy(1, k).wait_recv(), 1)
         x_turned[...] = x_cols[t].reshape(batch, x_width).T
 
-        def values_of(k, t=t):
-            c = peer(k)
+        def values_of(j, half, t=t):
+            c = beside(j, half)
             if t >= 2:
                 value_copy(t - 2, c).wait_recv()
                 value_w[c] = value_w[c] + value_got[t - 2, c].astype(F32)
@@ -257,16 +436,33 @@
             )
             return (product * scale_in).astype(BF16)
 
-        def send_part(k, t=t, values_of=values_of):
-            part[k] = values_of(k)
-            part_copy(t, k).start()
+        def send_part(j, t=t, values_of=values_of):
+            part[j, 0] = values_of(j, 0)
+            part[j, 1] = values_of(j, 1)
+            part_copy(t, j).start()
 
         def forward(t=t, values_of=values_of, send_part=send_part):
-            each(send_part, 1)
-            part_got[t, 0] = values_of(0)
-
-        def add_dmixed(c, t=t):
+            each(send_part, 1, row)
+            part_got[t, 0, 0] = values_of(0, 0)
+            part_got[t, 0, 1] = values_of(0, 1)
+
+        def cross(t=t):
+            each(lambda j: part_copy(t, j).wait(), 1, row)
+            summed = part_got[t, 0, 1].astype(F32)
+            for j in range(1, row):
+                summed = summed + part_got[t, j, 1].astype(F32)
+            across[...] = summed.astype(BF16)
+            across_copy(t).start()
+
+        def pass_dvalues(t=t):
+            dv_copy(t, 0).wait_recv()
+            each(lambda j: dv_copy(t, row + j).start(), 1, row)
+
+        def add_dmixed(i, t=t):
+            c = i
             if t >= 2:
+                if t - 2 == slow_step and not values_lead:
+                    c = lax.rem(i + detour, peers)
                 output_copy(t - 2, c).wait_recv()
                 output_w[c] = output_w[c] + output_got[t - 2, c].astype(F32)
             effective = (output_w[c] * inverse[0:1, 0:o_cols]).astype(BF16)
@@ -279,12 +475,14 @@
             )
 
         def backward(t=t, add_dmixed=add_dmixed):
-            each(lambda k: cot_copy(t, k).wait_recv(), 1)
+            each(lambda j: cot_copy(t, j).wait_recv(), 1, row)
+            each(lambda j: cot_copy(t, row + j).wait_recv(), 1, row)
             total[...] = jnp.zeros_like(total)
             each(add_dmixed)
             dmixed = (total[...] * scale_mid).astype(BF16)
             dvalues_all[t, f] = by_heads(mix_turned, dmixed)
-            each(lambda k: dv_copy(t, k).start(), 1)
+            dv_copy(t, 0).start()
+            each(lambda j: dv_copy(t, j).start(), 1, row)
 
         def update_output(c, t=t, slot=slot):
             cot = cot_all[t, :, :, pl.ds(pl.multiple_of(c * o_cols, o_cols), o_cols)]
@@ -296,49 +494,68 @@
             if t >= 2:
                 output_copy(t - 2, c).wait_send()
             output_msg[slot, c] = half.astype(BF16)
-            output_copy(t, c).start()
+            send_prompt(t, False, c)
 
         def outputs(t=t, update_output=update_output):
-            each(lambda k: part_copy(t, k).wait(), 1)
-            summed = part_got[t, 0].astype(F32)
-            for k in range(1, peers):
-                summed = summed + part_got[t, k].astype(F32)
+            summed = part_got[t, 0, 0].astype(F32)
+            for j in range(1, row):
+                summed = summed + part_got[t, j, 0].astype(F32)
+            across_copy(t).wait()
+            summed = summed + across_got[t].astype(F32)
             mixed_turned[...] = by_heads(mix, summed.astype(BF16)).T
             each(update_output)
 
-        def update_value(j, t=t, slot=slot):
-            c = peer(j)
+        def update_value(p, t=t, slot=slot):
+            c = chunk_at(p)
             grad = jnp.dot(x_turned[...], dvalues_all[t, c], preferred_element_type=F32)
             half = 0.5 * value_w[c] - (0.25 * scale_in) * grad
             value_w[c] = half
             if t >= 2:
                 value_copy(t - 2, c).wait_send()
             value_msg[slot, c] = half.astype(BF16)
-            value_copy(t, c).start()
-
-        def update_other(j, t=t, update_value=update_value):
-            dv_copy(t, peers - j).wait_recv()
-            update_value(j)
+            send_prompt(t, True, p)
+
+        def update_other(p, t=t, update_value=update_value):
+            dv_copy(t, row * lax.rem(p, 2) + row - 1 - p // 2).wait_recv()
+            update_value(p)
 
         def values(t=t, update_value=update_value, update_other=update_other):
-            each(update_other, 1)
-            update_value(0)
+            each(update_other, 0, peers - 2)
+            each(update_value, peers - 2)
 
         half_mass = mass * 0.5
         if t < 2:
             forward()
             backward()
+            if t >= 1:
+                send_later(t - 1, 1)
+            cross()
+            pass_dvalues()
         else:
             backward()
             forward()
+            send_later(t - 1, 1)
+            pass_dvalues()
+            cross()
         if t + 1 < steps:
-            each(lambda k: cot_copy(t + 1, k).start(), 1)
+            cot_lead(t + 1)
+        if t >= 1:
+            send_later(t - 1, 2)
         if t < 2:
             outputs()
             values()
         else:
             values()
             outputs()
+        if t + 1 < steps:
+            cot_pass(t + 1)
+        for earlier in range(steps):
+            if t == min(earlier + 1, steps - 1):
+                if earlier == slow_step:
+                    pass_relay()
+                for i in range(2):
+                    if earlier == side_step(i):
+                        pass_side(i)
         mass_msg[t] = half_mass.astype(BF16)
         mass_copy(t).start()
         mass = half_mass
@@ -366,8 +583,9 @@
             load_sem.at[1, c],
         )
 
-    def finish_value(j):
-        c = peer(j)
+    def finish_value(i):
+        p = lax.rem(i + detour, peers) if values_lead else i
+        c = chunk_at(p)
         value_copy(last - 1, c).wait()
         value_copy(last, c).wait_recv()
         result = (
@@ -385,18 +603,30 @@
         output_msg[0, c] = (result * inverse[0:1, 0:o_cols]).astype(BF16)
         output_store(c).start()
 
-    each(finish_value, 1)
-    finish_value(0)
+    each(finish_value)
     each(finish_output)
 
     def settle(k):
         x_copy(0, k).wait_send()
         x_copy(1, k).wait_send()
+
+    each(settle, 1)
+
+    def settle_row(j):
         for t in range(steps):
-            cot_copy(t, k).wait_send()
-            dv_copy(t, k).wait_send()
-
-    each(settle, 1)
+            cot_copy(t, j).wait_send()
+            cot_copy(t, row + j).wait_send()
+            dv_copy(t, j).wait_send()
+            dv_copy(t, row + j).wait_send()
+
+    each(settle_row, 1, row)
+    for t in range(steps):
+        cot_copy(t, 0).wait_send()
+        dv_copy(t, 0).wait_send()
+
+    each(lambda p: from_relay(p).wait_send(), 0, detour)
+    at_side(0, lambda p: from_side(0, p).wait_send())
+    at_side(1, lambda p: from_side(1, p).wait_send())
 
     def settle_chunk(c):
         value_copy(last, c).wait_send()
@@ -423,6 +653,11 @@
     dma = pltpu.SemaphoreType.DMA
     hbm = pl.BlockSpec(memory_space=pl.ANY)
     vmem = pl.BlockSpec(memory_space=pltpu.VMEM)
+
+    def chunk_of(step):
+        return (rows, own_inner) if step % steps >= 2 else (own_inner, o_cols)
+
+    relay_shape = (max(max(DETOUR[first]), 1), *chunk_of(3 - first))
     sizes = (groups, peers, steps, positions, heads, head_size)
     return pl.pallas_call(
         functools.partial(window_kernel, first, sizes),
@@ -445,8 +680,13 @@
             pltpu.VMEM((steps, peers, rows, own_inner), BF16),
             pltpu.VMEM((steps, peers, own_inner, o_cols), BF16),
             pltpu.VMEM((steps, *mass.shape), BF16),
-            pltpu.VMEM((peers, batch, own_inner), BF16),
-            pltpu.VMEM((steps, peers, batch, own_inner), BF16),
+            pltpu.VMEM((peers // 2, 2, batch, own_inner), BF16),
+            pltpu.VMEM((steps, peers // 2, 2, batch, own_inner), BF16),
+            pltpu.VMEM((batch, own_inner), BF16),
+            pltpu.VMEM((steps, batch, own_inner), BF16),
+            pltpu.VMEM(relay_shape, BF16),
+            pltpu.VMEM((SIDE, *chunk_of(-first)), BF16),
+            pltpu.VMEM((SIDE, *chunk_of(1 - first)), BF16),
             pltpu.VMEM((steps, peers, batch, own_inner), BF16),
             pltpu.VMEM((heads, batch, batch), BF16),
             pltpu.VMEM((heads, batch, batch), BF16),
@@ -469,6 +709,12 @@
             dma((steps, peers)),
             dma((steps,)),
             dma((steps,)),
+            dma((steps,)),
+            dma((steps,)),
+            dma((peers,)),
+            dma((peers,)),
+            dma((2, peers)),
+            dma((2, peers)),
         ],
         compiler_params=pltpu.CompilerParams(
             collective_id=first, has_side_effects=True, vmem_limit_bytes=63 << 20

time: 597 us -> 459 us (0.77)
  the two profiles are of different devices: /device:TPU:26 before, /device:TPU:6 now
where the time goes in v3:
time: 459 us; the launch traced here: 451 us
  Pallas kernels  434 us (95%)
  loops' own time  8.92 us (2%)
  local copies, waits for them, and re-layouts  5.83 us (1%)
    pallas_call x1, Pallas kernels, run_window(): pl.pallas_call(functools.partial(window_kernel, first, sizes), out_shape=...  434 us

profile of v3, /device:TPU:6, one launch (start us, length us, event | category | flops | bytes accessed | tf_op | source)
XLA Modules:
  0.0 451.3 jit_solution(13066027566787638664)
XLA Ops:
  2.0 444.5 %conditional.1 = (bf16[1,512,2048]{2,1,0:T(8,128)(2,1)}, bf16[1,256,4096]{2,1,0:T(8,128)(2,1)}, f32[1]{0:T(128)}) conditional(s32[]{:T(128)} %clamp.3, (bf16[1,4,32,4096]{3,2,1,0:T(8,128)(2,1)}, bf16[1,4,32,4096]{3,2,1,0:T(8,128)(2,1)}, bf16[1,512,2048]{2,1,0:T(8,128)(2,1)}, bf16[1,256,4096]{2,1,0:T(8,128)(2,1)}, ...), branch_computations={%region_0.1_spmd, %region_1.2_spmd, %region_2.3_spmd, %region_3.4_... | conditional | bytes 32 | solution.py:730
  2.5 434.3 %window.5 = (bf16[1,512,2048]{2,1,0:T(8,128)(2,1)}, bf16[1,256,4096]{2,1,0:T(8,128)(2,1)}, f32[16,512]{1,0:T(8,128)}) custom-call(bf16[1,4,32,4096]{3,2,1,0:T(8,128)(2,1)} %get-tuple-element.70.inputs, bf16[1,4,32,4096]{3,2,1,0:T(8,128)(2,1)} %get-tuple-element.71.cotangent, bf16[1,512,2048]{2,1,0:T(8,128)(2,1)} %get-tuple-element.72.value_in, ...), custom_call_target="tpu_custom_call" | custom-call | tf_op jit(solution)/shard_map/cond/branch_1_fun/window/pallas_call | solution.py:662
  436.8 1.2 slice.10
  446.4 0.0 copy-start
  446.4 3.3 copy.30
  449.7 0.0 copy-done
  449.7 1.3 copy.31
  (1 shorter events, 0.0 us)
Async XLA Ops:
  446.4 3.3 copy-start

commit v4 on v3

--- a/solution.py
+++ b/solution.py
@@ -11,8 +11,10 @@
 DISTANCES = (1, 2, 4, 8)
 RELAY = 12
 SIDE = 8
-PACE = ((4, 6), (2, 3), (16, 16), (16, 16))
-DETOUR = ((4, 4), (4, 4), (4, 4), (4, 4))
+PACE = (((4, 6), (2, 3), (16, 16), (16, 16)), ((4, 6), (1, 2), (16, 16), (16, 16)), ((16, 16), (16, 16), (16, 16), (16, 16)), ((16, 16), (1, 2), (16, 16), (16, 16)))
+COT_OVER_Y = (2, 2, 2, 1)
+DV_OVER_Y = False
+DETOUR = ((4, 4), (4, 4), (5, 5), (4, 4))
 MESH = pl.DeviceIdType.MESH
 F32 = jnp.float32
 BF16 = jnp.bfloat16
@@ -147,19 +149,26 @@
             (g, peer(k)),
         )
 
-    def cot_copy(t, k):
-        block = beside(0, k // row)
-        to = beside(lax.rem(k, row)) if not isinstance(k, int) else beside(0, 1)
-        return remote(
-            cot_all.at[t, block],
-            cot_all.at[t, block],
-            cot_send.at[t, k],
-            cot_recv.at[t, k],
+    def second(held, t, j, send, recv, over_y):
+        block, to = beside(0, 1), beside(j)
+        if j == 2 and over_y:
+            block, to = beside(2), beside(0, 1)
+        return remote(
+            held.at[t, block],
+            held.at[t, block],
+            send.at[t, row + j],
+            recv.at[t, row + j],
             (g, to),
         )
 
+    def cot_second(t, j):
+        return second(cot_all, t, j, cot_send, cot_recv, t < COT_OVER_Y[first])
+
+    def dv_second(t, j):
+        return second(dvalues_all, t, j, dv_send, dv_recv, DV_OVER_Y)
+
     def cot_first(t, k):
-        to = beside(k) if not isinstance(k, int) else beside(0, 1)
+        to = beside(k) if not isinstance(k, int) or k else beside(0, 1)
         return remote(
             cotangent.at[0, t], cot_all.at[t, f], cot_send.at[t, k], cot_recv.at[t, k], (g, to)
         )
@@ -169,15 +178,17 @@
         each(lambda j: cot_first(t, j).start(), 1, row)
 
     def cot_pass(t):
-        cot_copy(t, 0).wait_recv()
-        each(lambda j: cot_copy(t, row + j).start(), 1, row)
-
-    def dv_copy(t, k):
-        block = beside(0, k // row)
-        to = beside(lax.rem(k, row)) if not isinstance(k, int) else beside(0, 1)
-        return remote(
-            dvalues_all.at[t, block],
-            dvalues_all.at[t, block],
+        cot_first(t, 0).wait_recv()
+        cot_second(t, 1).start()
+        cot_second(t, 3).start()
+        cot_first(t, 2).wait_recv()
+        cot_second(t, 2).start()
+
+    def dv_first(t, k):
+        to = beside(k) if not isinstance(k, int) or k else beside(0, 1)
+        return remote(
+            dvalues_all.at[t, f],
+            dvalues_all.at[t, f],
             dv_send.at[t, k],
             dv_recv.at[t, k],
             (g, to),
@@ -318,7 +329,7 @@
             copy.start()
 
     def span(t, values, point):
-        marks = PACE[(first + t) % 4] if t + 1 < steps else (2 * peers, 2 * peers)
+        marks = PACE[first][(first + t) % 4] if t + 1 < steps else (2 * peers, 2 * peers)
         marks = (0, *marks, 2 * peers)
         shift = 0 if values == (t >= 2) else peers
         return tuple(min(max(m - shift, 0), peers) for m in marks[point : point + 2])
@@ -372,7 +383,6 @@
 
     each(lambda k: x_copy(0, k).start(), 1)
     cot_lead(0)
-    each(lambda k: x_copy(1, k).start(), 1)
 
     for copy in loads():
         copy.wait()
@@ -455,8 +465,11 @@
             across_copy(t).start()
 
         def pass_dvalues(t=t):
-            dv_copy(t, 0).wait_recv()
-            each(lambda j: dv_copy(t, row + j).start(), 1, row)
+            dv_first(t, 0).wait_recv()
+            dv_second(t, 1).start()
+            dv_second(t, 3).start()
+            dv_first(t, 2).wait_recv()
+            dv_second(t, 2).start()
 
         def add_dmixed(i, t=t):
             c = i
@@ -475,14 +488,16 @@
             )
 
         def backward(t=t, add_dmixed=add_dmixed):
-            each(lambda j: cot_copy(t, j).wait_recv(), 1, row)
-            each(lambda j: cot_copy(t, row + j).wait_recv(), 1, row)
+            for j in (1, 3):
+                cot_first(t, j).wait_recv()
+            for j in (1, 2, 3):
+                cot_second(t, j).wait_recv()
             total[...] = jnp.zeros_like(total)
             each(add_dmixed)
             dmixed = (total[...] * scale_mid).astype(BF16)
             dvalues_all[t, f] = by_heads(mix_turned, dmixed)
-            dv_copy(t, 0).start()
-            each(lambda j: dv_copy(t, j).start(), 1, row)
+            dv_first(t, 0).start()
+            each(lambda j: dv_first(t, j).start(), 1, row)
 
         def update_output(c, t=t, slot=slot):
             cot = cot_all[t, :, :, pl.ds(pl.multiple_of(c * o_cols, o_cols), o_cols)]
@@ -516,7 +531,10 @@
             send_prompt(t, True, p)
 
         def update_other(p, t=t, update_value=update_value):
-            dv_copy(t, row * lax.rem(p, 2) + row - 1 - p // 2).wait_recv()
+            @pl.when(p != 2)
+            def _():
+                dv_first(t, row * lax.rem(p, 2) + row - 1 - p // 2).wait_recv()
+
             update_value(p)
 
         def values(t=t, update_value=update_value, update_other=update_other):
@@ -531,24 +549,34 @@
                 send_later(t - 1, 1)
             cross()
             pass_dvalues()
+        elif first != 3 and (first + t - 2) % 4 != 2:
+            forward()
+            backward()
+            send_later(t - 1, 1)
+            cross()
+            pass_dvalues()
         else:
             backward()
             forward()
             send_later(t - 1, 1)
             pass_dvalues()
             cross()
+        if t == 0:
+            each(lambda k: x_copy(1, k).start(), 1)
         if t + 1 < steps:
             cot_lead(t + 1)
         if t >= 1:
             send_later(t - 1, 2)
         if t < 2:
             outputs()
+        else:
+            values()
+        if t + 1 < steps:
+            cot_pass(t + 1)
+        if t < 2:
             values()
         else:
-            values()
             outputs()
-        if t + 1 < steps:
-            cot_pass(t + 1)
         for earlier in range(steps):
             if t == min(earlier + 1, steps - 1):
                 if earlier == slow_step:
@@ -603,8 +631,12 @@
         output_msg[0, c] = (result * inverse[0:1, 0:o_cols]).astype(BF16)
         output_store(c).start()
 
-    each(finish_value)
-    each(finish_output)
+    if first == 3:
+        each(finish_value)
+        each(finish_output)
+    else:
+        each(finish_output)
+        each(finish_value)
 
     def settle(k):
         x_copy(0, k).wait_send()
@@ -612,17 +644,13 @@
 
     each(settle, 1)
 
-    def settle_row(j):
-        for t in range(steps):
-            cot_copy(t, j).wait_send()
-            cot_copy(t, row + j).wait_send()
-            dv_copy(t, j).wait_send()
-            dv_copy(t, row + j).wait_send()
-
-    each(settle_row, 1, row)
     for t in range(steps):
-        cot_copy(t, 0).wait_send()
-        dv_copy(t, 0).wait_send()
+        for j in range(row):
+            cot_first(t, j).wait_send()
+            dv_first(t, j).wait_send()
+        for j in range(1, row):
+            cot_second(t, j).wait_send()
+            dv_second(t, j).wait_send()
 
     each(lambda p: from_relay(p).wait_send(), 0, detour)
     at_side(0, lambda p: from_side(0, p).wait_send())

time: 459 us -> 451 us (0.983); the launches traced: 451 us -> 455 us
  loops' own time: 8.92 us -> 15.5 us
    another operation x1, loops' own time: 8.92 us -> 15.5 us  [on_device(): lax.switch(step_index[0] % 4, [functools.partial(run_window, first) for f...]
where the time goes in v4:
time: 451 us; the launch traced here: 455 us
  Pallas kernels  431 us (96%)
  loops' own time  15.5 us (3%)
  local copies, waits for them, and re-layouts  5.83 us (1%)
    pallas_call x1, Pallas kernels, run_window(): pl.pallas_call(functools.partial(window_kernel, first, sizes), out_shape=...  431 us
    another operation x1, loops' own time, on_device(): lax.switch(step_index[0] % 4, [functools.partial(run_window, first) for f...  15.5 us

profile of v4, /device:TPU:6, one launch (start us, length us, event | category | flops | bytes accessed | tf_op | source)
XLA Modules:
  0.0 454.6 jit_solution(9880137400063601116)
XLA Ops:
  2.0 447.5 %conditional.1 = (bf16[1,512,2048]{2,1,0:T(8,128)(2,1)}, bf16[1,256,4096]{2,1,0:T(8,128)(2,1)}, f32[1]{0:T(128)}) conditional(s32[]{:T(128)} %clamp.3, (bf16[1,4,32,4096]{3,2,1,0:T(8,128)(2,1)}, bf16[1,4,32,4096]{3,2,1,0:T(8,128)(2,1)}, bf16[1,512,2048]{2,1,0:T(8,128)(2,1)}, bf16[1,256,4096]{2,1,0:T(8,128)(2,1)}, ...), branch_computations={%region_0.1_spmd, %region_1.2_spmd, %region_2.3_spmd, %region_3.4_... | conditional | bytes 32 | solution.py:758
  2.0 430.8 %window.4 = (bf16[1,512,2048]{2,1,0:T(8,128)(2,1)}, bf16[1,256,4096]{2,1,0:T(8,128)(2,1)}, f32[16,512]{1,0:T(8,128)}) custom-call(bf16[1,4,32,4096]{3,2,1,0:T(8,128)(2,1)} %get-tuple-element.61.inputs, bf16[1,4,32,4096]{3,2,1,0:T(8,128)(2,1)} %get-tuple-element.62.cotangent, bf16[1,512,2048]{2,1,0:T(8,128)(2,1)} %get-tuple-element.63.value_in, ...), custom_call_target="tpu_custom_call" | custom-call | tf_op jit(solution)/shard_map/cond/branch_0_fun/window/pallas_call | solution.py:690
  432.8 1.2 slice.9
  449.5 0.0 copy-start
  449.5 3.3 copy.30
  452.8 0.0 copy-done
  452.8 1.3 copy.31
  (1 shorter events, 0.0 us)
Async XLA Ops:
  449.5 3.3 copy-start
